TPU v7x, 512 devices: a whole 4x4x16 slice. The times are simulated.
512 devices in a mesh: gx: 16 (over z), gy: 32 (over x, y, core).
Axes of the slice: x: 4, y: 4, z: 16, core: 2. Of those that a mesh axis runs over, the one named last changes fastest.
Arguments:
- defect: float32 [256, 1024, 128], P('gx', 'gy'), may hold values from -6 to 6
- coefficient: float32 [256, 1024, 128], P('gx', 'gy'), may hold values from 0.2 to 2
Outputs:
- correction: float32 [256, 1024, 128], P('gx', 'gy')
All inputs are finite; a program needn't handle non-finite values.
Results may differ from a plain program's by a relative error of at most 0.00002.
Values sent between devices are 32-bit elements; how exact they have to be, the bound alone decides.
A program may use at most 64 MiB of HBM per device.

v0:
```python
import jax
import jax.numpy as jnp
from jax import lax
from jax.sharding import PartitionSpec as P

LEVELS = 7
SWEEPS = 2
COARSE_SWEEPS = 8


damping = 0.7
directions = ((1, 0, 0), (-1, 0, 0), (0, 1, 0), (0, -1, 0), (0, 0, 1), (0, 0, -1))


def with_halo(block, sides, width):
    for axis, dim in sides:
        count = lax.axis_size(axis)
        forward = [(i, i + 1) for i in range(count - 1)]
        backward = [(target, source) for source, target in forward]
        low = lax.ppermute(
            lax.slice_in_dim(block, block.shape[dim] - width, None, axis=dim), axis, forward
        )
        high = lax.ppermute(lax.slice_in_dim(block, 0, width, axis=dim), axis, backward)
        block = jnp.concatenate([low, block, high], axis=dim)
    return block


def neighbour(padded, offset):
    extent = padded.shape
    return padded[
        1 + offset[0] : extent[0] - 1 + offset[0],
        1 + offset[1] : extent[1] - 1 + offset[1],
        1 + offset[2] : extent[2] - 1 + offset[2],
    ]


def stencil(padded, coefficient, factor):
    extended = jnp.pad(padded, ((0, 0), (0, 0), (1, 1)))
    conduct = jnp.pad(coefficient, ((0, 0), (0, 0), (1, 1)))
    centre = neighbour(extended, (0, 0, 0))
    centre_coeff = neighbour(conduct, (0, 0, 0))
    fluxes = jnp.zeros_like(centre)
    weights = jnp.zeros_like(centre)
    for offset in directions:
        face = 0.5 * factor * (centre_coeff + neighbour(conduct, offset))
        fluxes = fluxes + face * (centre - neighbour(extended, offset))
        weights = weights + face
    return (fluxes, weights)


def coarsen(values):
    summed = values[0::2] + values[1::2]
    summed = summed[:, 0::2] + summed[:, 1::2]
    summed = summed[:, :, 0::2] + summed[:, :, 1::2]
    return 0.125 * summed


def prolong(values):
    return jnp.repeat(jnp.repeat(jnp.repeat(values, 2, 0), 2, 1), 2, 2)


def pad_sides(values):
    return jnp.pad(values, ((1, 1), (1, 1), (0, 0)))


def jacobi_whole(iterate, source, padded_coeff, factor):
    applied, diagonal = stencil(pad_sides(iterate), padded_coeff, factor)
    return iterate + damping * (source - applied) / diagonal


def whole_cycle(source, coefficient, degree):
    factor = 0.25**degree
    padded_coeff = pad_sides(coefficient)
    iterate = jnp.zeros_like(source)
    if degree == LEVELS - 1:
        for sweep_no in range(COARSE_SWEEPS):
            iterate = jacobi_whole(iterate, source, padded_coeff, factor)
        return iterate
    for sweep_no in range(SWEEPS):
        iterate = jacobi_whole(iterate, source, padded_coeff, factor)
    applied = stencil(pad_sides(iterate), padded_coeff, factor)[0]
    coarse = whole_cycle(coarsen(source - applied), coarsen(coefficient), degree + 1)
    iterate = iterate + prolong(coarse)
    for sweep_no in range(SWEEPS):
        iterate = jacobi_whole(iterate, source, padded_coeff, factor)
    return iterate


def face_rim(iterate):
    return with_halo(iterate, (("gx", 0), ("gy", 1)), 1)


def jacobi_local(iterate, source, padded_coeff, factor):
    applied, diagonal = stencil(face_rim(iterate), padded_coeff, factor)
    return iterate + damping * (source - applied) / diagonal


def smooth_level(iterate, source, padded_coeff, factor):
    for sweep_no in range(SWEEPS):
        iterate = jacobi_local(iterate, source, padded_coeff, factor)
    return iterate


def body(defect, coefficient):
    split = 3
    source = defect
    conduct = coefficient
    history = []
    for degree in range(split):
        factor = 0.25**degree
        padded_coeff = with_halo(conduct, (("gx", 0), ("gy", 1)), 1)
        coeff_deep = padded_coeff
        source_deep = source
        iterate = smooth_level(jnp.zeros_like(source), source, padded_coeff, factor)
        applied = stencil(face_rim(iterate), padded_coeff, factor)[0]
        history.append((iterate, source, padded_coeff, coeff_deep, source_deep, factor))
        source = coarsen(source - applied)
        conduct = coarsen(conduct)
    stacked = jnp.stack([source, conduct])
    gathered_y = lax.all_gather(stacked, "gy", axis=2, tiled=True)
    entire = lax.all_gather(gathered_y, "gx", axis=1, tiled=True)
    coarse_whole = whole_cycle(entire[0], entire[1], split)
    extent = source.shape
    start_z = jnp.zeros((), jnp.int32)
    coarse = lax.dynamic_slice(
        coarse_whole,
        (lax.axis_index("gx") * extent[0], lax.axis_index("gy") * extent[1], start_z),
        extent,
    )
    for degree in reversed(range(split)):
        iterate, source, padded_coeff, coeff_deep, source_deep, factor = history[degree]
        iterate = iterate + prolong(coarse)
        coarse = smooth_level(iterate, source, padded_coeff, factor)
    return coarse


def solution(mesh):
    placed = (P("gx", "gy", None), P("gx", "gy", None))
    return jax.shard_map(
        body, mesh=mesh, in_specs=placed, out_specs=P("gx", "gy", None), check_vma=False
    )
```

profile of v0, /device:TPU:132, one launch (start us, length us, event | category | flops | bytes accessed | tf_op | source)
XLA Modules:
  0.0 467.4 jit_solution(5792163973641666667)
XLA Ops:
  2.0 3.8 collective-permute-start.3
  5.9 3.2 collective-permute-start.17
  12.5 3.8 collective-permute-start.2
  21.6 3.2 collective-permute-start
  24.8 3.4 collective-permute-done
  28.2 3.4 collective-permute-start.16
  36.1 5.3 %collective-permute-start.5 = (f32[18,1,128]{2,1,0:T(1,128)S(1)}, f32[18,1,128]{2,1,0:T(1,128)S(1)}, u32[]{:S(2)}, u32[]{:S(2)}) collective-permute-start(f32[18,1,128]{2,1,0:T(1,128)S(1)} %get-tuple-element.66), channel_id=1, source_target_pairs={{1,0},{2,1},{3,2},{4,3},{5,4},{6,5},{7,6},{8,7},{9,8},{10,9},{11,1... | collective-permute-start | bytes 27656 | tf_op jit(solution)/shard_map/ppermute | solution.py:23
  43.7 4.0 collective-permute-start.18
  53.8 3.9 collective-permute-start.9
  57.8 3.6 collective-permute-start.35
  61.4 3.5 collective-permute-start.32
  64.9 4.1 collective-permute-start.10
  71.0 5.8 %collective-permute-start.20 = (f32[10,1,64]{2,1,0:T(1,128)S(1)}, f32[10,1,64]{2,1,0:T(1,128)S(1)}, u32[]{:S(2)}, u32[]{:S(2)}) collective-permute-start(f32[10,1,64]{2,1,0:T(1,128)S(1)} %get-tuple-element.87), channel_id=1, source_target_pairs={{1,0},{2,1},{3,2},{4,3},{5,4},{6,5},{7,6},{8,7},{9,8},{10,9},{11,1... | collective-permute-start | bytes 7688 | tf_op jit(solution)/shard_map/ppermute | solution.py:23
  83.8 3.2 collective-permute-start.13
  87.1 3.5 collective-permute-start.21
  92.6 5.8 %collective-permute-start.14 = (f32[18,1,128]{2,1,0:T(1,128)S(1)}, f32[18,1,128]{2,1,0:T(1,128)S(1)}, u32[]{:S(2)}, u32[]{:S(2)}) collective-permute-start(f32[18,1,128]{2,1,0:T(1,128)S(1)} %get-tuple-element.60), channel_id=1, source_target_pairs={{1,0},{2,1},{3,2},{4,3},{5,4},{6,5},{7,6},{8,7},{9,8},{10,9},{11,1... | collective-permute-start | bytes 27656 | tf_op jit(solution)/shard_map/ppermute | solution.py:23
  100.4 4.4 collective-permute-start.34
  108.8 3.4 collective-permute-start.24
  115.2 3.8 collective-permute-start.36
  121.0 5.8 %collective-permute-start.26 = (f32[10,1,64]{2,1,0:T(1,128)S(1)}, f32[10,1,64]{2,1,0:T(1,128)S(1)}, u32[]{:S(2)}, u32[]{:S(2)}) collective-permute-start(f32[10,1,64]{2,1,0:T(1,128)S(1)} %get-tuple-element.85), channel_id=1, source_target_pairs={{1,0},{2,1},{3,2},{4,3},{5,4},{6,5},{7,6},{8,7},{9,8},{10,9},{11,1... | collective-permute-start | bytes 7688 | tf_op jit(solution)/shard_map/ppermute | solution.py:23
  128.7 5.8 %collective-permute-start.37 = (f32[6,1,32]{2,1,0:T(1,128)S(1)}, f32[6,1,32]{2,1,0:T(1,128)S(1)}, u32[]{:S(2)}, u32[]{:S(2)}) collective-permute-start(f32[6,1,32]{2,1,0:T(1,128)S(1)} %get-tuple-element.111), channel_id=1, source_target_pairs={{1,0},{2,1},{3,2},{4,3},{5,4},{6,5},{7,6},{8,7},{9,8},{10,9},{11,1... | collective-permute-start | bytes 2312 | tf_op jit(solution)/shard_map/ppermute | solution.py:23
  136.7 3.9 collective-permute-start.28
  143.6 3.7 collective-permute-done.29
  147.4 4.3 collective-permute-start.30
  153.8 5.0 %collective-permute-done.31 = f32[10,1,64]{2,1,0:T(1,128)S(1)} collective-permute-done((f32[10,1,64]{2,1,0:T(1,128)S(1)}, f32[10,1,64]{2,1,0:T(1,128)S(1)}, u32[]{:S(2)}, u32[]{:S(2)}) %collective-permute-start.31) | collective-permute-done | bytes 2592 | tf_op jit(solution)/shard_map/ppermute | solution.py:20
  161.6 3.9 collective-permute-start.41
  172.7 4.6 collective-permute-done.43
  179.5 3.9 collective-permute-start.45
  191.4 4.6 collective-permute-done.47
  196.6 23.2 %all_gather.6 = f32[2,2,128,16]{3,1,0,2:T(2,128)S(1)} all-gather(f32[2,2,4,16]{3,1,0,2:T(2,128)S(1)} %copy.752), channel_id=1, replica_groups=mesh['gx'=16,'gy'=32] {'gy'}, dimensions={2}, use_global_device_ids=true | all-gather | bytes 33792 | tf_op jit(solution)/shard_map/all_gather | solution.py:120
  219.8 32.5 %all_gather.7 = f32[2,32,128,16]{2,3,0,1:T(8,128)S(1)} all-gather(f32[2,2,128,16]{2,3,0,1:T(8,128)S(1)} %copy.753), channel_id=1, replica_groups=mesh['gx'=16,'gy'=32] {'gx'}, dimensions={1}, use_global_device_ids=true | all-gather | bytes 557056 | tf_op jit(solution)/shard_map/all_gather | solution.py:121
  262.8 3.7 slice.2041
  266.6 3.8 slice.2042
  275.1 3.7 slice.2047
  278.8 3.8 slice.2048
  359.0 3.9 collective-permute-done.49
  367.4 4.8 %collective-permute-done.51 = f32[6,1,32]{2,1,0:T(1,128)S(1)} collective-permute-done((f32[6,1,32]{2,1,0:T(1,128)S(1)}, f32[6,1,32]{2,1,0:T(1,128)S(1)}, u32[]{:S(2)}, u32[]{:S(2)}) %collective-permute-start.51) | collective-permute-done | bytes 800 | tf_op jit(solution)/shard_map/ppermute | solution.py:20
  375.2 3.1 collective-permute-start.53
  378.4 3.6 collective-permute-done.53
  386.3 4.6 collective-permute-done.55
  393.4 3.9 collective-permute-start.57
  404.7 4.6 collective-permute-done.59
  415.6 3.6 collective-permute-done.61
  423.5 4.6 collective-permute-done.63
  431.3 3.9 collective-permute-start.65
  442.7 4.7 collective-permute-done.67
  450.1 3.9 collective-permute-start.69
  461.3 4.7 collective-permute-done.71
  (560 shorter events, 219.6 us)
Async XLA Ops:
  0.0 31.7 %collective-permute-start.1 = (f32[1,32,128]{2,1,0:T(8,128)S(1)}, f32[1,32,128]{2,1,0:T(8,128)S(1)}, u32[]{:S(2)}, u32[]{:S(2)}) collective-permute-start(f32[1,32,128]{2,1,0:T(8,128)S(1)} %broadcast.315), channel_id=1, source_target_pairs={{32,0},{64,32},{96,64},{128,96},{160,128},{192,160},{224,192},{256... | collective-permute-start | bytes 49160 | tf_op jit(solution)/shard_map/ppermute | solution.py:23
  2.0 31.6 %collective-permute-start.3 = (f32[1,32,128]{2,1,0:T(8,128)S(1)}, f32[1,32,128]{2,1,0:T(8,128)S(1)}, u32[]{:S(2)}, u32[]{:S(2)}) collective-permute-start(f32[1,32,128]{2,1,0:T(8,128)S(1)} %broadcast.315), channel_id=1, source_target_pairs={{0,32},{32,64},{64,96},{96,128},{128,160},{160,192},{192,224},{224... | collective-permute-start | bytes 49160 | tf_op jit(solution)/shard_map/ppermute | solution.py:20
  5.9 59.0 %collective-permute-start.17 = (f32[1,16,64]{2,1,0:T(8,128)S(1)}, f32[1,16,64]{2,1,0:T(8,128)S(1)}, u32[]{:S(2)}, u32[]{:S(2)}) collective-permute-start(f32[1,16,64]{2,1,0:T(8,128)S(1)} %broadcast.318), channel_id=1, source_target_pairs={{32,0},{64,32},{96,64},{128,96},{160,128},{192,160},{224,192},{256... | collective-permute-start | bytes 12296 | tf_op jit(solution)/shard_map/ppermute | solution.py:23
  9.1 59.9 %collective-permute-start.19 = (f32[1,16,64]{2,1,0:T(8,128)S(1)}, f32[1,16,64]{2,1,0:T(8,128)S(1)}, u32[]{:S(2)}, u32[]{:S(2)}) collective-permute-start(f32[1,16,64]{2,1,0:T(8,128)S(1)} %broadcast.318), channel_id=1, source_target_pairs={{0,32},{32,64},{64,96},{96,128},{128,160},{160,192},{192,224},{224... | collective-permute-start | bytes 12296 | tf_op jit(solution)/shard_map/ppermute | solution.py:20
  12.5 9.1 %collective-permute-start.2 = (f32[1,32,128]{2,1,0:T(8,128)S(1)}, f32[1,32,128]{2,1,0:T(8,128)S(1)}, u32[]{:S(2)}, u32[]{:S(2)}) collective-permute-start(f32[1,32,128]{2,1,0:T(8,128)S(1)} %get-tuple-element.76), channel_id=1, source_target_pairs={{0,32},{32,64},{64,96},{96,128},{128,160},{160,192},{192,224},{224... | collective-permute-start | bytes 49160 | tf_op jit(solution)/shard_map/ppermute | solution.py:20
  28.2 23.6 %collective-permute-start.16 = (f32[1,16,64]{2,1,0:T(8,128)S(1)}, f32[1,16,64]{2,1,0:T(8,128)S(1)}, u32[]{:S(2)}, u32[]{:S(2)}) collective-permute-start(f32[1,16,64]{2,1,0:T(8,128)S(1)} %get-tuple-element.99), channel_id=1, source_target_pairs={{32,0},{64,32},{96,64},{128,96},{160,128},{192,160},{224,192},{256... | collective-permute-start | bytes 12296 | tf_op jit(solution)/shard_map/ppermute | solution.py:23
  33.6 7.8 %collective-permute-start.6 = (f32[18,1,128]{2,1,0:T(1,128)S(1)}, f32[18,1,128]{2,1,0:T(1,128)S(1)}, u32[]{:S(2)}, u32[]{:S(2)}) collective-permute-start(f32[18,1,128]{2,1,0:T(1,128)S(1)} %get-tuple-element.63), channel_id=1, source_target_pairs={{0,1},{1,2},{2,3},{3,4},{4,5},{5,6},{6,7},{7,8},{8,9},{9,10},{10,1... | collective-permute-start | bytes 27656 | tf_op jit(solution)/shard_map/ppermute | solution.py:20
  36.1 7.6 %collective-permute-start.5 = (f32[18,1,128]{2,1,0:T(1,128)S(1)}, f32[18,1,128]{2,1,0:T(1,128)S(1)}, u32[]{:S(2)}, u32[]{:S(2)}) collective-permute-start(f32[18,1,128]{2,1,0:T(1,128)S(1)} %get-tuple-element.66), channel_id=1, source_target_pairs={{1,0},{2,1},{3,2},{4,3},{5,4},{6,5},{7,6},{8,7},{9,8},{10,9},{11,1... | collective-permute-start | bytes 27656 | tf_op jit(solution)/shard_map/ppermute | solution.py:23
  41.4 7.1 %collective-permute-start.7 = (f32[18,1,128]{2,1,0:T(1,128)S(1)}, f32[18,1,128]{2,1,0:T(1,128)S(1)}, u32[]{:S(2)}, u32[]{:S(2)}) collective-permute-start(f32[18,1,128]{2,1,0:T(1,128)S(1)} %get-tuple-element.65), channel_id=1, source_target_pairs={{0,1},{1,2},{2,3},{3,4},{4,5},{5,6},{6,7},{7,8},{8,9},{9,10},{10,1... | collective-permute-start | bytes 27656 | tf_op jit(solution)/shard_map/ppermute | solution.py:20
  43.7 10.1 %collective-permute-start.18 = (f32[1,16,64]{2,1,0:T(8,128)S(1)}, f32[1,16,64]{2,1,0:T(8,128)S(1)}, u32[]{:S(2)}, u32[]{:S(2)}) collective-permute-start(f32[1,16,64]{2,1,0:T(8,128)S(1)} %get-tuple-element.98), channel_id=1, source_target_pairs={{0,32},{32,64},{64,96},{96,128},{128,160},{160,192},{192,224},{224... | collective-permute-start | bytes 12296 | tf_op jit(solution)/shard_map/ppermute | solution.py:20
  48.5 78.3 %collective-permute-start.33 = (f32[1,8,32]{2,1,0:T(8,128)S(1)}, f32[1,8,32]{2,1,0:T(8,128)S(1)}, u32[]{:S(2)}, u32[]{:S(2)}) collective-permute-start(f32[1,8,32]{2,1,0:T(8,128)S(1)} %broadcast.322), channel_id=1, source_target_pairs={{32,0},{64,32},{96,64},{128,96},{160,128},{192,160},{224,192},{256... | collective-permute-start | bytes 3080 | tf_op jit(solution)/shard_map/ppermute | solution.py:23
  53.8 7.6 %collective-permute-start.9 = (f32[1,32,128]{2,1,0:T(8,128)S(1)}, f32[1,32,128]{2,1,0:T(8,128)S(1)}, u32[]{:S(2)}, u32[]{:S(2)}) collective-permute-start(f32[1,32,128]{2,1,0:T(8,128)S(1)} %get-tuple-element.74), channel_id=1, source_target_pairs={{0,32},{32,64},{64,96},{96,128},{128,160},{160,192},{192,224},{224... | collective-permute-start | bytes 49160 | tf_op jit(solution)/shard_map/ppermute | solution.py:20
  57.8 70.9 %collective-permute-start.35 = (f32[1,8,32]{2,1,0:T(8,128)S(1)}, f32[1,8,32]{2,1,0:T(8,128)S(1)}, u32[]{:S(2)}, u32[]{:S(2)}) collective-permute-start(f32[1,8,32]{2,1,0:T(8,128)S(1)} %broadcast.322), channel_id=1, source_target_pairs={{0,32},{32,64},{64,96},{96,128},{128,160},{160,192},{192,224},{224... | collective-permute-start | bytes 3080 | tf_op jit(solution)/shard_map/ppermute | solution.py:20
  61.4 50.8 %collective-permute-start.32 = (f32[1,8,32]{2,1,0:T(8,128)S(1)}, f32[1,8,32]{2,1,0:T(8,128)S(1)}, u32[]{:S(2)}, u32[]{:S(2)}) collective-permute-start(f32[1,8,32]{2,1,0:T(8,128)S(1)} %get-tuple-element.125), channel_id=1, source_target_pairs={{32,0},{64,32},{96,64},{128,96},{160,128},{192,160},{224,192},{256... | collective-permute-start | bytes 3080 | tf_op jit(solution)/shard_map/ppermute | solution.py:23
  69.0 7.7 %collective-permute-start.11 = (f32[18,1,128]{2,1,0:T(1,128)S(1)}, f32[18,1,128]{2,1,0:T(1,128)S(1)}, u32[]{:S(2)}, u32[]{:S(2)}) collective-permute-start(f32[18,1,128]{2,1,0:T(1,128)S(1)} %get-tuple-element.61), channel_id=1, source_target_pairs={{0,1},{1,2},{2,3},{3,4},{4,5},{5,6},{6,7},{7,8},{8,9},{9,10},{10,1... | collective-permute-start | bytes 27656 | tf_op jit(solution)/shard_map/ppermute | solution.py:20
  71.0 8.4 %collective-permute-start.20 = (f32[10,1,64]{2,1,0:T(1,128)S(1)}, f32[10,1,64]{2,1,0:T(1,128)S(1)}, u32[]{:S(2)}, u32[]{:S(2)}) collective-permute-start(f32[10,1,64]{2,1,0:T(1,128)S(1)} %get-tuple-element.87), channel_id=1, source_target_pairs={{1,0},{2,1},{3,2},{4,3},{5,4},{6,5},{7,6},{8,7},{9,8},{10,9},{11,1... | collective-permute-start | bytes 7688 | tf_op jit(solution)/shard_map/ppermute | solution.py:23
  76.7 7.0 %collective-permute-start.22 = (f32[10,1,64]{2,1,0:T(1,128)S(1)}, f32[10,1,64]{2,1,0:T(1,128)S(1)}, u32[]{:S(2)}, u32[]{:S(2)}) collective-permute-start(f32[10,1,64]{2,1,0:T(1,128)S(1)} %get-tuple-element.86), channel_id=1, source_target_pairs={{0,1},{1,2},{2,3},{3,4},{4,5},{5,6},{6,7},{7,8},{8,9},{9,10},{10,1... | collective-permute-start | bytes 7688 | tf_op jit(solution)/shard_map/ppermute | solution.py:20
  79.4 7.7 %collective-permute-start.12 = (f32[1,32,128]{2,1,0:T(8,128)S(1)}, f32[1,32,128]{2,1,0:T(8,128)S(1)}, u32[]{:S(2)}, u32[]{:S(2)}) collective-permute-start(f32[1,32,128]{2,1,0:T(8,128)S(1)} %get-tuple-element.73), channel_id=1, source_target_pairs={{32,0},{64,32},{96,64},{128,96},{160,128},{192,160},{224,192},{256... | collective-permute-start | bytes 49160 | tf_op jit(solution)/shard_map/ppermute | solution.py:23
  83.8 6.9 %collective-permute-start.13 = (f32[1,32,128]{2,1,0:T(8,128)S(1)}, f32[1,32,128]{2,1,0:T(8,128)S(1)}, u32[]{:S(2)}, u32[]{:S(2)}) collective-permute-start(f32[1,32,128]{2,1,0:T(8,128)S(1)} %get-tuple-element.72), channel_id=1, source_target_pairs={{0,32},{32,64},{64,96},{96,128},{128,160},{160,192},{192,224},{224... | collective-permute-start | bytes 49160 | tf_op jit(solution)/shard_map/ppermute | solution.py:20
  90.6 7.7 %collective-permute-start.23 = (f32[10,1,64]{2,1,0:T(1,128)S(1)}, f32[10,1,64]{2,1,0:T(1,128)S(1)}, u32[]{:S(2)}, u32[]{:S(2)}) collective-permute-start(f32[10,1,64]{2,1,0:T(1,128)S(1)} %get-tuple-element.88), channel_id=1, source_target_pairs={{0,1},{1,2},{2,3},{3,4},{4,5},{5,6},{6,7},{7,8},{8,9},{9,10},{10,1... | collective-permute-start | bytes 7688 | tf_op jit(solution)/shard_map/ppermute | solution.py:20
  92.6 7.8 %collective-permute-start.14 = (f32[18,1,128]{2,1,0:T(1,128)S(1)}, f32[18,1,128]{2,1,0:T(1,128)S(1)}, u32[]{:S(2)}, u32[]{:S(2)}) collective-permute-start(f32[18,1,128]{2,1,0:T(1,128)S(1)} %get-tuple-element.60), channel_id=1, source_target_pairs={{1,0},{2,1},{3,2},{4,3},{5,4},{6,5},{7,6},{8,7},{9,8},{10,9},{11,1... | collective-permute-start | bytes 27656 | tf_op jit(solution)/shard_map/ppermute | solution.py:23
  98.4 7.1 %collective-permute-start.15 = (f32[18,1,128]{2,1,0:T(1,128)S(1)}, f32[18,1,128]{2,1,0:T(1,128)S(1)}, u32[]{:S(2)}, u32[]{:S(2)}) collective-permute-start(f32[18,1,128]{2,1,0:T(1,128)S(1)} %get-tuple-element.59), channel_id=1, source_target_pairs={{0,1},{1,2},{2,3},{3,4},{4,5},{5,6},{6,7},{7,8},{8,9},{9,10},{10,1... | collective-permute-start | bytes 27656 | tf_op jit(solution)/shard_map/ppermute | solution.py:20
  100.4 14.7 %collective-permute-start.34 = (f32[1,8,32]{2,1,0:T(8,128)S(1)}, f32[1,8,32]{2,1,0:T(8,128)S(1)}, u32[]{:S(2)}, u32[]{:S(2)}) collective-permute-start(f32[1,8,32]{2,1,0:T(8,128)S(1)} %get-tuple-element.124), channel_id=1, source_target_pairs={{0,32},{32,64},{64,96},{96,128},{128,160},{160,192},{192,224},{224... | collective-permute-start | bytes 3080 | tf_op jit(solution)/shard_map/ppermute | solution.py:20
  108.8 10.2 %collective-permute-start.24 = (f32[1,16,64]{2,1,0:T(8,128)S(1)}, f32[1,16,64]{2,1,0:T(8,128)S(1)}, u32[]{:S(2)}, u32[]{:S(2)}) collective-permute-start(f32[1,16,64]{2,1,0:T(8,128)S(1)} %get-tuple-element.97), channel_id=1, source_target_pairs={{32,0},{64,32},{96,64},{128,96},{160,128},{192,160},{224,192},{256... | collective-permute-start | bytes 12296 | tf_op jit(solution)/shard_map/ppermute | solution.py:23
  112.2 8.7 %collective-permute-start.25 = (f32[1,16,64]{2,1,0:T(8,128)S(1)}, f32[1,16,64]{2,1,0:T(8,128)S(1)}, u32[]{:S(2)}, u32[]{:S(2)}) collective-permute-start(f32[1,16,64]{2,1,0:T(8,128)S(1)} %get-tuple-element.96), channel_id=1, source_target_pairs={{0,32},{32,64},{64,96},{96,128},{128,160},{160,192},{192,224},{224... | collective-permute-start | bytes 12296 | tf_op jit(solution)/shard_map/ppermute | solution.py:20
  115.2 25.4 %collective-permute-start.36 = (f32[6,1,32]{2,1,0:T(1,128)S(1)}, f32[6,1,32]{2,1,0:T(1,128)S(1)}, u32[]{:S(2)}, u32[]{:S(2)}) collective-permute-start(f32[6,1,32]{2,1,0:T(1,128)S(1)} %get-tuple-element.109), channel_id=1, source_target_pairs={{1,0},{2,1},{3,2},{4,3},{5,4},{6,5},{7,6},{8,7},{9,8},{10,9},{11,1... | collective-permute-start | bytes 2312 | tf_op jit(solution)/shard_map/ppermute | solution.py:23
  119.0 24.5 %collective-permute-start.38 = (f32[6,1,32]{2,1,0:T(1,128)S(1)}, f32[6,1,32]{2,1,0:T(1,128)S(1)}, u32[]{:S(2)}, u32[]{:S(2)}) collective-permute-start(f32[6,1,32]{2,1,0:T(1,128)S(1)} %get-tuple-element.108), channel_id=1, source_target_pairs={{0,1},{1,2},{2,3},{3,4},{4,5},{5,6},{6,7},{7,8},{8,9},{9,10},{10,1... | collective-permute-start | bytes 2312 | tf_op jit(solution)/shard_map/ppermute | solution.py:20
  121.0 13.5 %collective-permute-start.26 = (f32[10,1,64]{2,1,0:T(1,128)S(1)}, f32[10,1,64]{2,1,0:T(1,128)S(1)}, u32[]{:S(2)}, u32[]{:S(2)}) collective-permute-start(f32[10,1,64]{2,1,0:T(1,128)S(1)} %get-tuple-element.85), channel_id=1, source_target_pairs={{1,0},{2,1},{3,2},{4,3},{5,4},{6,5},{7,6},{8,7},{9,8},{10,9},{11,1... | collective-permute-start | bytes 7688 | tf_op jit(solution)/shard_map/ppermute | solution.py:23
  126.7 9.7 %collective-permute-start.27 = (f32[10,1,64]{2,1,0:T(1,128)S(1)}, f32[10,1,64]{2,1,0:T(1,128)S(1)}, u32[]{:S(2)}, u32[]{:S(2)}) collective-permute-start(f32[10,1,64]{2,1,0:T(1,128)S(1)} %get-tuple-element.84), channel_id=1, source_target_pairs={{0,1},{1,2},{2,3},{3,4},{4,5},{5,6},{6,7},{7,8},{8,9},{9,10},{10,1... | collective-permute-start | bytes 7688 | tf_op jit(solution)/shard_map/ppermute | solution.py:20
  128.7 24.9 %collective-permute-start.37 = (f32[6,1,32]{2,1,0:T(1,128)S(1)}, f32[6,1,32]{2,1,0:T(1,128)S(1)}, u32[]{:S(2)}, u32[]{:S(2)}) collective-permute-start(f32[6,1,32]{2,1,0:T(1,128)S(1)} %get-tuple-element.111), channel_id=1, source_target_pairs={{1,0},{2,1},{3,2},{4,3},{5,4},{6,5},{7,6},{8,7},{9,8},{10,9},{11,1... | collective-permute-start | bytes 2312 | tf_op jit(solution)/shard_map/ppermute | solution.py:23
  134.5 19.2 %collective-permute-start.39 = (f32[6,1,32]{2,1,0:T(1,128)S(1)}, f32[6,1,32]{2,1,0:T(1,128)S(1)}, u32[]{:S(2)}, u32[]{:S(2)}) collective-permute-start(f32[6,1,32]{2,1,0:T(1,128)S(1)} %get-tuple-element.110), channel_id=1, source_target_pairs={{0,1},{1,2},{2,3},{3,4},{4,5},{5,6},{6,7},{7,8},{8,9},{9,10},{10,1... | collective-permute-start | bytes 2312 | tf_op jit(solution)/shard_map/ppermute | solution.py:20
  136.7 6.9 %collective-permute-start.28 = (f32[1,16,64]{2,1,0:T(8,128)S(1)}, f32[1,16,64]{2,1,0:T(8,128)S(1)}, u32[]{:S(2)}, u32[]{:S(2)}) collective-permute-start(f32[1,16,64]{2,1,0:T(8,128)S(1)} %get-tuple-element.95), channel_id=1, source_target_pairs={{32,0},{64,32},{96,64},{128,96},{160,128},{192,160},{224,192},{256... | collective-permute-start | bytes 12296 | tf_op jit(solution)/shard_map/ppermute | solution.py:23
  140.6 6.8 %collective-permute-start.29 = (f32[1,16,64]{2,1,0:T(8,128)S(1)}, f32[1,16,64]{2,1,0:T(8,128)S(1)}, u32[]{:S(2)}, u32[]{:S(2)}) collective-permute-start(f32[1,16,64]{2,1,0:T(8,128)S(1)} %get-tuple-element.94), channel_id=1, source_target_pairs={{0,32},{32,64},{64,96},{96,128},{128,160},{160,192},{192,224},{224... | collective-permute-start | bytes 12296 | tf_op jit(solution)/shard_map/ppermute | solution.py:20
  151.7 7.0 %collective-permute-start.31 = (f32[10,1,64]{2,1,0:T(1,128)S(1)}, f32[10,1,64]{2,1,0:T(1,128)S(1)}, u32[]{:S(2)}, u32[]{:S(2)}) collective-permute-start(f32[10,1,64]{2,1,0:T(1,128)S(1)} %get-tuple-element.82), channel_id=1, source_target_pairs={{0,1},{1,2},{2,3},{3,4},{4,5},{5,6},{6,7},{7,8},{8,9},{9,10},{10,1... | collective-permute-start | bytes 7688 | tf_op jit(solution)/shard_map/ppermute | solution.py:20
  170.3 7.0 %collective-permute-start.43 = (f32[6,1,32]{2,1,0:T(1,128)S(1)}, f32[6,1,32]{2,1,0:T(1,128)S(1)}, u32[]{:S(2)}, u32[]{:S(2)}) collective-permute-start(f32[6,1,32]{2,1,0:T(1,128)S(1)} %get-tuple-element.106), channel_id=1, source_target_pairs={{0,1},{1,2},{2,3},{3,4},{4,5},{5,6},{6,7},{7,8},{8,9},{9,10},{10,1... | collective-permute-start | bytes 2312 | tf_op jit(solution)/shard_map/ppermute | solution.py:20
  177.5 9.5 %collective-permute-start.44 = (f32[1,8,32]{2,1,0:T(8,128)S(1)}, f32[1,8,32]{2,1,0:T(8,128)S(1)}, u32[]{:S(2)}, u32[]{:S(2)}) collective-permute-start(f32[1,8,32]{2,1,0:T(8,128)S(1)} %get-tuple-element.121), channel_id=1, source_target_pairs={{32,0},{64,32},{96,64},{128,96},{160,128},{192,160},{224,192},{256... | collective-permute-start | bytes 3080 | tf_op jit(solution)/shard_map/ppermute | solution.py:23
  179.5 7.6 %collective-permute-start.45 = (f32[1,8,32]{2,1,0:T(8,128)S(1)}, f32[1,8,32]{2,1,0:T(8,128)S(1)}, u32[]{:S(2)}, u32[]{:S(2)}) collective-permute-start(f32[1,8,32]{2,1,0:T(8,128)S(1)} %get-tuple-element.120), channel_id=1, source_target_pairs={{0,32},{32,64},{64,96},{96,128},{128,160},{160,192},{192,224},{224... | collective-permute-start | bytes 3080 | tf_op jit(solution)/shard_map/ppermute | solution.py:20
  189.0 7.0 %collective-permute-start.47 = (f32[6,1,32]{2,1,0:T(1,128)S(1)}, f32[6,1,32]{2,1,0:T(1,128)S(1)}, u32[]{:S(2)}, u32[]{:S(2)}) collective-permute-start(f32[6,1,32]{2,1,0:T(1,128)S(1)} %get-tuple-element.104), channel_id=1, source_target_pairs={{0,1},{1,2},{2,3},{3,4},{4,5},{5,6},{6,7},{7,8},{8,9},{9,10},{10,1... | collective-permute-start | bytes 2312 | tf_op jit(solution)/shard_map/ppermute | solution.py:20
  365.1 7.2 %collective-permute-start.51 = (f32[6,1,32]{2,1,0:T(1,128)S(1)}, f32[6,1,32]{2,1,0:T(1,128)S(1)}, u32[]{:S(2)}, u32[]{:S(2)}) collective-permute-start(f32[6,1,32]{2,1,0:T(1,128)S(1)} %get-tuple-element.102), channel_id=1, source_target_pairs={{0,1},{1,2},{2,3},{3,4},{4,5},{5,6},{6,7},{7,8},{8,9},{9,10},{10,1... | collective-permute-start | bytes 2312 | tf_op jit(solution)/shard_map/ppermute | solution.py:20
  383.9 7.0 %collective-permute-start.55 = (f32[6,1,32]{2,1,0:T(1,128)S(1)}, f32[6,1,32]{2,1,0:T(1,128)S(1)}, u32[]{:S(2)}, u32[]{:S(2)}) collective-permute-start(f32[6,1,32]{2,1,0:T(1,128)S(1)} %get-tuple-element.100), channel_id=1, source_target_pairs={{0,1},{1,2},{2,3},{3,4},{4,5},{5,6},{6,7},{7,8},{8,9},{9,10},{10,1... | collective-permute-start | bytes 2312 | tf_op jit(solution)/shard_map/ppermute | solution.py:20
  393.4 6.8 %collective-permute-start.57 = (f32[1,16,64]{2,1,0:T(8,128)S(1)}, f32[1,16,64]{2,1,0:T(8,128)S(1)}, u32[]{:S(2)}, u32[]{:S(2)}) collective-permute-start(f32[1,16,64]{2,1,0:T(8,128)S(1)} %get-tuple-element.92), channel_id=1, source_target_pairs={{0,32},{32,64},{64,96},{96,128},{128,160},{160,192},{192,224},{224... | collective-permute-start | bytes 12296 | tf_op jit(solution)/shard_map/ppermute | solution.py:20
  402.2 7.2 %collective-permute-start.59 = (f32[10,1,64]{2,1,0:T(1,128)S(1)}, f32[10,1,64]{2,1,0:T(1,128)S(1)}, u32[]{:S(2)}, u32[]{:S(2)}) collective-permute-start(f32[10,1,64]{2,1,0:T(1,128)S(1)} %get-tuple-element.80), channel_id=1, source_target_pairs={{0,1},{1,2},{2,3},{3,4},{4,5},{5,6},{6,7},{7,8},{8,9},{9,10},{10,1... | collective-permute-start | bytes 7688 | tf_op jit(solution)/shard_map/ppermute | solution.py:20
  412.4 6.8 %collective-permute-start.61 = (f32[1,16,64]{2,1,0:T(8,128)S(1)}, f32[1,16,64]{2,1,0:T(8,128)S(1)}, u32[]{:S(2)}, u32[]{:S(2)}) collective-permute-start(f32[1,16,64]{2,1,0:T(8,128)S(1)} %get-tuple-element.90), channel_id=1, source_target_pairs={{0,32},{32,64},{64,96},{96,128},{128,160},{160,192},{192,224},{224... | collective-permute-start | bytes 12296 | tf_op jit(solution)/shard_map/ppermute | solution.py:20
  421.1 7.0 %collective-permute-start.63 = (f32[10,1,64]{2,1,0:T(1,128)S(1)}, f32[10,1,64]{2,1,0:T(1,128)S(1)}, u32[]{:S(2)}, u32[]{:S(2)}) collective-permute-start(f32[10,1,64]{2,1,0:T(1,128)S(1)} %get-tuple-element.78), channel_id=1, source_target_pairs={{0,1},{1,2},{2,3},{3,4},{4,5},{5,6},{6,7},{7,8},{8,9},{9,10},{10,1... | collective-permute-start | bytes 7688 | tf_op jit(solution)/shard_map/ppermute | solution.py:20
  431.3 6.8 %collective-permute-start.65 = (f32[1,32,128]{2,1,0:T(8,128)S(1)}, f32[1,32,128]{2,1,0:T(8,128)S(1)}, u32[]{:S(2)}, u32[]{:S(2)}) collective-permute-start(f32[1,32,128]{2,1,0:T(8,128)S(1)} %get-tuple-element.69), channel_id=1, source_target_pairs={{0,32},{32,64},{64,96},{96,128},{128,160},{160,192},{192,224},{224... | collective-permute-start | bytes 49160 | tf_op jit(solution)/shard_map/ppermute | solution.py:20
  440.2 7.2 %collective-permute-start.67 = (f32[18,1,128]{2,1,0:T(1,128)S(1)}, f32[18,1,128]{2,1,0:T(1,128)S(1)}, u32[]{:S(2)}, u32[]{:S(2)}) collective-permute-start(f32[18,1,128]{2,1,0:T(1,128)S(1)} %get-tuple-element.57), channel_id=1, source_target_pairs={{0,1},{1,2},{2,3},{3,4},{4,5},{5,6},{6,7},{7,8},{8,9},{9,10},{10,1... | collective-permute-start | bytes 27656 | tf_op jit(solution)/shard_map/ppermute | solution.py:20
  450.1 6.8 %collective-permute-start.69 = (f32[1,32,128]{2,1,0:T(8,128)S(1)}, f32[1,32,128]{2,1,0:T(8,128)S(1)}, u32[]{:S(2)}, u32[]{:S(2)}) collective-permute-start(f32[1,32,128]{2,1,0:T(8,128)S(1)} %get-tuple-element.67), channel_id=1, source_target_pairs={{0,32},{32,64},{64,96},{96,128},{128,160},{160,192},{192,224},{224... | collective-permute-start | bytes 49160 | tf_op jit(solution)/shard_map/ppermute | solution.py:20
  458.9 7.1 %collective-permute-start.71 = (f32[18,1,128]{2,1,0:T(1,128)S(1)}, f32[18,1,128]{2,1,0:T(1,128)S(1)}, u32[]{:S(2)}, u32[]{:S(2)}) collective-permute-start(f32[18,1,128]{2,1,0:T(1,128)S(1)} %get-tuple-element.55), channel_id=1, source_target_pairs={{0,1},{1,2},{2,3},{3,4},{4,5},{5,6},{6,7},{7,8},{8,9},{9,10},{10,1... | collective-permute-start | bytes 27656 | tf_op jit(solution)/shard_map/ppermute | solution.py:20
  (125 other events, 1452.7 us)
where the time goes:
time: 473 us; the launch traced here: 467 us
  starting transfers between devices  212 us (45%)
  local copies, waits for them, and re-layouts  88.1 us (19%)
  waiting for transfers between devices  74.9 us (16%)
  blocking collectives  55.7 us (12%)
  other arithmetic  34.4 us (7%)
    ppermute x36, starting transfers between devices, with_halo(): lax.ppermute(lax.slice_in_dim(block, 0, width, axis=dim), axis, backward)  109 us
    ppermute x36, starting transfers between devices, with_halo(): lax.ppermute(lax.slice_in_dim(block, block.shape[dim] - width, None, axis...  103 us
    ppermute x36, waiting for transfers between devices, with_halo(): lax.ppermute(lax.slice_in_dim(block, block.shape[dim] - width, None, axis...  71.4 us
    all_gather x1, blocking collectives, body(): entire = lax.all_gather(gathered_y, 'gx', axis=1, tiled=True)  32.5 us
    slice x24, local copies, waits for them, and re-layouts, coarsen(): summed = summed[:, 0::2] + summed[:, 1::2]  27.5 us
    all_gather x1, blocking collectives, body(): gathered_y = lax.all_gather(stacked, 'gy', axis=2, tiled=True)  23.2 us
    slice x12, local copies, waits for them, and re-layouts, coarsen(): summed = values[0::2] + values[1::2]  17.4 us
    unnamed x206, local copies, waits for them, and re-layouts  13.5 us
  transfers between devices with their start and end apart: 72, of which 21 were waited for; matrix products, arithmetic and copies ran while one was open for 3% of the time, Pallas kernels for 0%

commit v1 on v0

v1 whole, which is shorter than its diff:
```python
import functools

import jax
import jax.numpy as jnp
from jax import lax
from jax.experimental import pallas as pl
from jax.experimental.pallas import tpu as pltpu
from jax.sharding import PartitionSpec as P

MESH = pl.DeviceIdType.MESH
DAMP = 0.7
KEEP = 0.3
COARSE_SWEEPS = 8
LANES = 128
f32 = jnp.float32

BX, BY = (16, 8, 4), (32, 16, 8)
HX, HY = (4, 8, 4), (4, 8, 4)
EX = tuple(b + 2 * h for b, h in zip(BX, HX))
EY = tuple(b + 2 * h for b, h in zip(BY, HY))

NEAR = [(a, b) for a in (-1, 0, 1) for b in (-1, 0, 1) if (a, b) != (0, 0)]


def ahead(t, d):
    return pltpu.roll(t, (-d) % LANES, axis=t.ndim - 1)


def rows_ahead(t, d):
    n = t.shape[-2]
    return pltpu.roll(t, (-d) % n, axis=t.ndim - 2)


def planes_ahead(t, d):
    d = d % t.shape[0]
    return jnp.concatenate([t[d:], t[:d]], axis=0) if d else t


def lane_iota(shape):
    return lax.broadcasted_iota(jnp.int32, shape, len(shape) - 1)


def bit(lane, b):
    return (lane & (1 << b)) != 0


def swap(t, b):
    on = bit(lane_iota(t.shape), b)
    return jnp.where(on, ahead(t, -(1 << b)), ahead(t, 1 << b))


def spread(t, b, value):
    on = bit(lane_iota(t.shape), b)
    if value:
        return jnp.where(on, t, ahead(t, 1 << b))
    return jnp.where(on, ahead(t, -(1 << b)), t)


def loop(lo, hi, body, unroll=1):
    def step(i, c):
        body(i)
        return c

    lax.fori_loop(lo, hi, step, 0, unroll=unroll)


class Block:
    def __init__(self, level, gx, gy, nx, ny, refs):
        self.level = level
        self.factor = 0.25**level
        self.zs = 1 << level
        self.bx, self.by, self.hx, self.hy = BX[level], BY[level], HX[level], HY[level]
        self.ex, self.ey = EX[level], EY[level]
        self.gx, self.gy, self.nx, self.ny = gx, gy, nx, ny
        self.k, self.s, self.va, self.vb, self.wx, self.wy, self.wz, self.inv, self.dg = refs
        shape = (self.ey, LANES)
        self.lane = lane_iota(shape)
        y = gy * self.by - self.hy + lax.broadcasted_iota(jnp.int32, shape, 0)
        self.row_in = jnp.where((y >= 0) & (y < ny * self.by), 1.0, 0.0).astype(f32)

    def inside(self, x):
        gx = self.gx * self.bx - self.hx + x
        return self.row_in * jnp.where((gx >= 0) & (gx < self.nx * self.bx), 1.0, 0.0).astype(f32)

    def weights(self, lo, hi, unroll=1):
        half = 0.5 * self.factor
        last = self.lane >= LANES - self.zs
        first = self.lane < self.zs

        def step(x, carry):
            kc, fxm = carry
            m = self.inside(x)
            kn = self.k[x + 1] * self.inside(x + 1)
            fxp = half * (kc + kn)
            fyp = half * (kc + rows_ahead(kc, 1))
            fzp = half * (kc + jnp.where(last, 0.0, ahead(kc, self.zs)))
            wz = jnp.where(last, 0.0, fzp)
            fzm = jnp.where(first, half * kc, ahead(wz, -self.zs))
            diag = ((fxm + fxp) + (rows_ahead(fyp, -1) + fyp)) + (fzp + fzm)
            self.wx[x] = fxp
            self.wy[x] = fyp
            self.wz[x] = wz
            self.dg[x] = diag
            self.inv[x] = jnp.where(m > 0, DAMP / diag, 0.0)
            return kn, fxp

        k0 = self.k[lo - 1] * self.inside(lo - 1)
        k1 = self.k[lo] * self.inside(lo)
        self.wx[lo - 1] = half * (k0 + k1)
        lax.fori_loop(lo, hi, step, (k1, half * (k0 + k1)), unroll=unroll)

    def first(self, src, dst, lo, hi, unroll=1):
        def step(x):
            dst[x] = self.inv[x] * src[x]

        loop(lo, hi, step, unroll)

    def pull(self, v, x):
        c = v[x]
        wy, wz = self.wy[x], self.wz[x]
        t = self.wx[x] * v[x + 1] + self.wx[x - 1] * v[x - 1]
        u = wy * rows_ahead(c, 1) + rows_ahead(wy * c, -1)
        w = wz * ahead(c, self.zs) + ahead(wz * c, -self.zs)
        return c, (t + u) + w

    def sweep(self, s, src, dst, lo, hi, unroll=1, shift=0):
        def step(x):
            c, near = self.pull(src, x)
            dst[x - shift] = KEEP * c + self.inv[x] * (s[x] + near)

        loop(lo, hi, step, unroll)

    def residual(self, s, v, x):
        c, near = self.pull(v, x)
        return (s[x] - self.dg[x] * c) + near

    def restrict(self, plane, tmp, lo, pairs, row, count, put, unroll=1):
        lane = lane_iota((count, LANES))

        def step(i):
            x = lo + 2 * i
            t = plane(x) + plane(x + 1)
            tmp[i, pl.ds(0, t.shape[0]), :] = t
            t = tmp[i, pl.ds(row, count, stride=2), :] + tmp[i, pl.ds(row + 1, count, stride=2), :]
            put(i, 0.125 * (t + swap(t, self.level)))

        loop(0, pairs, step, unroll)

    def slabs(self, ref, wx, wy):
        parts = []
        for dx, dy in NEAR:
            spans = []
            for d, h, b, w in ((dx, self.hx, self.bx, wx), (dy, self.hy, self.by, wy)):
                if d == 0:
                    spans.append((h, h, b))
                elif d > 0:
                    spans.append((h + b - w, h - w, w))
                else:
                    spans.append((h, h + b, w))
            (sx, tx, cx), (sy, ty, cy) = spans
            parts.append(
                (
                    ref.at[pl.ds(sx, cx), pl.ds(sy, cy), :],
                    ref.at[pl.ds(tx, cx), pl.ds(ty, cy), :],
                )
            )
        return parts


class Whole:
    def __init__(self, factor, k, near, masks, inside):
        half = 0.5 * factor
        self.near = near
        diag = None
        self.w = []
        for n, mask in zip(near(k), masks):
            face = half * (k + n)
            self.w.append(jnp.where(mask, face, 0.0))
            face = jnp.where(mask, face, half * k)
            diag = face if diag is None else diag + face
        self.diag = diag
        inv = DAMP / diag
        self.inv = inv if inside is None else jnp.where(inside, inv, 0.0)

    def pull(self, v):
        total = None
        for n, w in zip(self.near(v), self.w):
            total = w * n if total is None else total + w * n
        return total

    def sweep(self, s, v):
        return KEEP * v + self.inv * (s + self.pull(v))

    def residual(self, s, v):
        return (s - self.diag * v) + self.pull(v)


def kernel(nx, ny, *refs):
    s_in, k_in, out = refs[:3]
    level_refs = [refs[3 + 9 * l : 12 + 9 * l] for l in range(3)]
    (
        tmp, rep, sv2, pack, acc, halo3, v3s, bcc, own4, v4s,
        local_sem, s0_sems, r0_sems, s1_sems, r1_sems, s2_sems, r2_sems,
        sa_sem, ra_sem, sh_sems, rh_sems, sb_sem, rb_sem,
    ) = refs[30:]
    gx, gy = lax.axis_index("gx"), lax.axis_index("gy")
    gh = nx // 8

    def there(dx, dy):
        return (lax.rem(gx + dx + nx, nx), lax.rem(gy + dy + ny, ny))

    L = [Block(l, gx, gy, nx, ny, level_refs[l]) for l in range(3)]
    l0, l1, l2 = L
    own0 = (pl.ds(HX[0], BX[0]), pl.ds(HY[0], BY[0]))
    loads = [
        pltpu.make_async_copy(k_in, l0.k.at[own0[0], own0[1], :], local_sem.at[0]),
        pltpu.make_async_copy(s_in, l0.s.at[own0[0], own0[1], :], local_sem.at[1]),
    ]
    for c in loads:
        c.start()

    column = [(i, j) for i in range(nx) for j in (-1, 0, 1) if (i, j) != (0, 0)]
    line = [(0, j) for j in range(1, ny)]
    column.sort(key=lambda o: -min(o[0], nx - o[0]))
    peers = column + [(0, j) for j in range(2, ny - 1)]
    acc[...] = jnp.zeros_like(acc)
    v3s[...] = jnp.zeros_like(v3s)
    barrier = pltpu.get_barrier_semaphore()
    for dx, dy in peers:
        pl.semaphore_signal(barrier, inc=1, device_id=there(dx, dy), device_id_type=MESH)
    for c in loads:
        c.wait()

    def put_k1(i, t):
        l1.k[HX[1] + i, pl.ds(HY[1], BY[1]), :] = t

    l0.restrict(lambda x: l0.k[x, own0[1], :], tmp, HX[0], BX[1], 0, BY[1], put_k1)

    pl.semaphore_wait(barrier, len(peers))

    pending = []

    def send(parts, ssems, rsems, base=0):
        copies = []
        for i, (dx, dy) in enumerate(NEAR):
            src, dst = parts[i]
            c = pltpu.make_async_remote_copy(
                src, dst, ssems.at[base + i], rsems.at[base + i], device_id=there(dx, dy), device_id_type=MESH
            )
            c.start()
            copies.append(c)
        pending.extend(copies)
        return copies

    got_k0 = send(l0.slabs(l0.k, 4, 4), s0_sems, r0_sems, 0)
    got_s0 = send(l0.slabs(l0.s, 3, 3), s0_sems, r0_sems, 8)
    got_k1 = send(l1.slabs(l1.k, 8, 8), s1_sems, r1_sems, 0)

    for c in got_k0:
        c.wait_recv()
    l0.weights(1, EX[0] - 1)
    for c in got_s0:
        c.wait_recv()
    l0.first(l0.s, l0.va, 1, EX[0] - 1)
    l0.sweep(l0.s, l0.va, l0.vb, 2, EX[0] - 2)

    def put_s1(i, t):
        l1.s[HX[1] + i, pl.ds(HY[1], BY[1]), :] = t

    l0.restrict(lambda x: l0.residual(l0.s, l0.vb, x), tmp, HX[0], BX[1], HY[0], BY[1], put_s1)
    got_s1 = send(l1.slabs(l1.s, 6, 8), s1_sems, r1_sems, 8)

    for c in got_k1:
        c.wait_recv()

    def put_k2(i, t):
        l2.k[i] = t

    l1.restrict(lambda x: l1.k[x], tmp, 0, EX[2], 0, EY[2], put_k2)
    l1.weights(1, EX[1] - 1)
    l2.weights(1, EX[2] - 1)

    def packed(plane_ref):
        t = plane_ref[...]
        lane = lane_iota(t.shape)
        sub = lax.broadcasted_iota(jnp.int32, t.shape, 0)
        return jnp.sum(jnp.where((lane & 7) == sub, t, 0.0), axis=0, keepdims=True)

    def put_pack(i, t):
        pack[pl.ds(4 * i, 4), :] = t

    l2.restrict(lambda x: l2.k[x], tmp, HX[2], 2, HY[2], 4, put_pack, unroll=True)
    acc[1, gx, pl.ds(1, 1), :] = packed(pack)

    for c in got_s1:
        c.wait_recv()
    l1.first(l1.s, l1.va, 2, EX[1] - 2)
    l1.sweep(l1.s, l1.va, l1.vb, 3, EX[1] - 3)

    def put_s2(i, t):
        l2.s[2 + i] = t

    l1.restrict(lambda x: l1.residual(l1.s, l1.vb, x), tmp, 4, 8, 0, EY[2], put_s2)

    l2.first(l2.s, l2.va, 2, EX[2] - 2, unroll=True)
    l2.sweep(l2.s, l2.va, l2.vb, 3, EX[2] - 3, unroll=True)
    l2.restrict(lambda x: l2.residual(l2.s, l2.vb, x), tmp, HX[2], 2, HY[2], 4, put_pack, unroll=True)
    acc[0, gx, pl.ds(1, 1), :] = packed(pack)

    got_a = []
    for n, (dx, dy) in enumerate(column):
        c = pltpu.make_async_remote_copy(
            acc.at[:, gx, pl.ds(1, 1), :],
            acc.at[:, gx, pl.ds(1 - dy, 1), :],
            sa_sem.at[n],
            ra_sem.at[n],
            device_id=there(dx, dy),
            device_id_type=MESH,
        )
        c.start()
        got_a.append(c)

    own2 = (pl.ds(HX[2], BX[2]), pl.ds(HY[2], BY[2]))
    sv2[0, own2[0], own2[1], :] = l2.s[own2[0], own2[1], :]
    sv2[1, own2[0], own2[1], :] = l2.vb[own2[0], own2[1], :]
    got_sv = send(l2.slabs(sv2.at[0], 4, 4), s2_sems, r2_sems, 0)
    got_sv += send(l2.slabs(sv2.at[1], 4, 4), s2_sems, r2_sems, 8)

    for c in got_a:
        c.wait_recv()

    shape = (nx, 8, LANES)
    lane = lane_iota(shape)
    px = lax.broadcasted_iota(jnp.int32, shape, 0)
    py = gy - 1 + lax.broadcasted_iota(jnp.int32, shape, 1)
    b2, yl, z3 = bit(lane, 2), lane & 3, lane >> 3

    def near3(v):
        up, down = ahead(v, 4), ahead(v, -4)
        return (
            jnp.where(b2, planes_ahead(down, 1), up),
            jnp.where(b2, down, planes_ahead(up, -1)),
            jnp.where(yl == 3, rows_ahead(ahead(v, -3), 1), ahead(v, 1)),
            jnp.where(yl == 0, rows_ahead(ahead(v, 3), -1), ahead(v, -1)),
            ahead(v, 8),
            ahead(v, -8),
        )

    x3, y3 = 2 * px + jnp.where(b2, 1, 0), 4 * py + yl
    in3 = (py >= 0) & (py < ny) & (py < gy + 2)
    w3 = Whole(
        0.25**3,
        jnp.where(in3, acc[1], 0.0),
        near3,
        (x3 < 2 * nx - 1, x3 > 0, y3 < 4 * ny - 1, y3 > 0, z3 < 15, z3 > 0),
        in3,
    )
    s3 = acc[0]
    v = w3.inv * s3
    v = w3.sweep(s3, v)
    v3s[pl.ds(1, nx)] = v
    r3 = w3.residual(s3, v)

    def coarse4(t):
        t = t + swap(t, 2)
        t = t + swap(t, 0)
        t = 0.125 * (t + swap(t, 3))
        on0, on2, on3 = (bit(lane_iota((8, LANES)), b) for b in (0, 2, 3))
        rows = []
        for h in range(gh):
            p = [t[8 * h + i] for i in range(8)]
            p = [jnp.where(on0, p[2 * i + 1], p[2 * i]) for i in range(4)]
            p = [jnp.where(on2, p[2 * i + 1], p[2 * i]) for i in range(2)]
            rows.append(jnp.where(on3, p[1], p[0])[1:2])
        return rows

    mine = jnp.concatenate(coarse4(r3) + coarse4(acc[1]), axis=0)
    own4[pl.ds(0, 2 * gh), :] = mine
    bcc[pl.ds(pl.multiple_of(8 * gy, 8), 2 * gh), :] = mine
    got_b = []
    for n, (dx, dy) in enumerate(line):
        c = pltpu.make_async_remote_copy(
            own4.at[pl.ds(0, 2 * gh), :],
            bcc.at[pl.ds(pl.multiple_of(8 * gy, 8), 2 * gh), :],
            sb_sem.at[n],
            rb_sem.at[n],
            device_id=there(dx, dy),
            device_id_type=MESH,
        )
        c.start()
        got_b.append(c)
    got_h = []
    for n, dy in enumerate((1, -1)):
        c = pltpu.make_async_remote_copy(
            v3s.at[pl.ds(1, nx), pl.ds(1, 1), :],
            halo3.at[:, pl.ds(1 - dy, 1), :],
            sh_sems.at[n],
            rh_sems.at[n],
            device_id=there(0, dy),
            device_id_type=MESH,
        )
        c.start()
        got_h.append(c)
    for c in got_b:
        c.wait_recv()

    s4 = jnp.stack([bcc[pl.ds(h, ny, stride=8), :] for h in range(gh)])
    k4 = jnp.stack([bcc[pl.ds(gh + h, ny, stride=8), :] for h in range(gh)])
    shape = (gh, ny, LANES)
    lane = lane_iota(shape)
    top = lax.broadcasted_iota(jnp.int32, shape, 0)
    py = lax.broadcasted_iota(jnp.int32, shape, 1)
    b0, b1, low = bit(lane, 0), bit(lane, 1), lane & 13

    def near4(v):
        up, down = ahead(v, 2), ahead(v, -2)
        return (
            jnp.where(low == 13, planes_ahead(ahead(v, -13), 1), jnp.where(b0, ahead(v, 3), ahead(v, 1))),
            jnp.where(low == 0, planes_ahead(ahead(v, 13), -1), jnp.where(b0, ahead(v, -1), ahead(v, -3))),
            jnp.where(b1, rows_ahead(down, 1), up),
            jnp.where(b1, down, rows_ahead(up, -1)),
            ahead(v, 16),
            ahead(v, -16),
        )

    y4, z4 = 2 * py + jnp.where(b1, 1, 0), lane >> 4
    w4 = Whole(
        0.25**4,
        k4,
        near4,
        (
            (low < 13) | (top < gh - 1),
            (low > 0) | (top > 0),
            y4 < 2 * ny - 1,
            y4 > 0,
            z4 < 7,
            z4 > 0,
        ),
        None,
    )

    def coarse5(t):
        t = t + swap(t, 0)
        t = t + swap(t, 1)
        t = 0.125 * (t + swap(t, 4))
        if gh == 1:
            return t[0]
        return jnp.where(bit(lane_iota((ny, LANES)), 0), t[1], t[0])

    shape = (ny, LANES)
    lane = lane_iota(shape)
    row = lax.broadcasted_iota(jnp.int32, shape, 0)
    mid, z5, z6 = lane & 12, lane >> 5, lane >> 6
    c0, c3 = bit(lane, 0), bit(lane, 3)
    end_hi = c0 if gh == 2 else lane >= 0
    end_lo = ~c0 if gh == 2 else lane >= 0

    def near5(v):
        return (
            jnp.where(mid == 12, ahead(v, -11), ahead(v, 4)),
            jnp.where(mid == 0, ahead(v, 11), ahead(v, -4)),
            rows_ahead(v, 1),
            rows_ahead(v, -1),
            ahead(v, 32),
            ahead(v, -32),
        )

    def near6(v):
        return (
            jnp.where(c3, ahead(v, -7), ahead(v, 8)),
            jnp.where(c3, ahead(v, -8), ahead(v, 7)),
            rows_ahead(v, 2),
            rows_ahead(v, -2),
            ahead(v, 64),
            ahead(v, -64),
        )

    k5 = coarse5(k4)
    w5 = Whole(
        0.25**5,
        k5,
        near5,
        (~((mid == 12) & end_hi), ~((mid == 0) & end_lo), row < ny - 1, row > 0, z5 < 3, z5 > 0),
        None,
    )

    def coarse6(t):
        t = t + swap(t, 2)
        t = t + swap(t, 5)
        odd = (row & 1) != 0
        return 0.125 * (t + jnp.where(odd, rows_ahead(t, -1), rows_ahead(t, 1)))

    w6 = Whole(
        0.25**6,
        coarse6(k5),
        near6,
        (~(c3 & end_hi), ~((~c3) & end_lo), row < ny - 2, row > 1, z6 < 1, z6 > 0),
        None,
    )

    v4 = w4.inv * s4
    v4 = w4.sweep(s4, v4)
    s5 = coarse5(w4.residual(s4, v4))
    v5 = w5.inv * s5
    v5 = w5.sweep(s5, v5)
    s6 = coarse6(w5.residual(s5, v5))
    v6 = w6.inv * s6
    v6 = lax.fori_loop(0, COARSE_SWEEPS - 1, lambda i, t: w6.sweep(s6, t), v6)
    v5 = v5 + v6
    v5 = w5.sweep(s5, v5)
    v5 = w5.sweep(s5, v5)
    if gh == 1:
        v4 = v4 + v5[None]
    else:
        v4 = v4 + jnp.stack([spread(v5, 0, 0), spread(v5, 0, 1)])
    v4 = w4.sweep(s4, v4)
    v4 = w4.sweep(s4, v4)
    v4s[:, pl.ds(8, ny), :] = v4

    for c in got_h:
        c.wait_recv()
    planes = []
    for h in range(gh):
        t = [v4s[h, pl.ds(7 + gy, 8), :]]
        for b in (3, 2, 0):
            t = [spread(q, b, value) for q in t for value in (0, 1)]
        planes += t
    sub = lax.broadcasted_iota(jnp.int32, (nx, 8, LANES), 1)
    v = jnp.where(sub == 1, v3s[pl.ds(1, nx)], halo3[...]) + jnp.stack(planes)
    v = jnp.where(in3, v, 0.0)
    v = w3.sweep(s3, v)
    v = w3.sweep(s3, v)
    for c in got_h:
        c.wait_send()
    v3s[pl.ds(1, nx)] = v

    for c in got_sv:
        c.wait_recv()
    shape = (8, LANES)
    lane, sub = lane_iota(shape), lax.broadcasted_iota(jnp.int32, shape, 0)
    for d in range(3):
        t = v3s[gx + d]
        rows = [jnp.broadcast_to(t[i : i + 1], shape) for i in range(3)]
        rows = jnp.where(sub < 2, rows[0], jnp.where(sub < 6, rows[1], rows[2]))
        for xl in range(2):
            t = jnp.where((lane & 7) == 4 * xl + ((sub + 2) & 3), rows, 0.0)
            for b in range(3):
                t = t + swap(t, b)
            n = 2 * d + xl
            rep[n, pl.ds(0, 8, stride=2), :] = t
            rep[n, pl.ds(1, 8, stride=2), :] = t
            t = rep[n, pl.ds(0, EY[2]), :]
            for e in range(2):
                x = 2 * n + e
                l2.va[x] = jnp.where(l2.inside(x) > 0, sv2[1, x] + t, 0.0)
    l2.sweep(sv2.at[0], l2.va, l2.vb, 1, EX[2] - 1, unroll=True)
    l2.sweep(sv2.at[0], l2.vb, l2.va, 2, EX[2] - 2, unroll=True)

    def up1(i):
        t = l2.va[i + 2]
        rep[i, pl.ds(0, EY[2], stride=2), :] = t
        rep[i, pl.ds(1, EY[2], stride=2), :] = t
        t = rep[i, pl.ds(0, EY[1]), :]
        for e in range(2):
            x = 2 * i + 4 + e
            l1.va[x] = l1.vb[x] + t

    loop(0, 8, up1)
    l1.sweep(l1.s, l1.va, l1.vb, 6, EX[1] - 6)
    l1.sweep(l1.s, l1.vb, l1.va, 7, EX[1] - 7)

    def up0(i):
        t = l1.va[i + 7]
        rep[i, pl.ds(4, EY[1], stride=2), :] = t
        rep[i, pl.ds(5, EY[1], stride=2), :] = t
        t = rep[i, pl.ds(16, EY[0]), :]
        for e in range(2):
            x = 2 * i + 2 + e
            l0.va[x] = l0.vb[x] + t

    loop(0, 10, up0)
    l0.sweep(l0.s, l0.va, l0.vb, 3, EX[0] - 3)
    l0.sweep(l0.s, l0.vb, l0.va, 4, EX[0] - 4)
    c = pltpu.make_async_copy(l0.va.at[own0[0], own0[1], :], out, local_sem.at[0])
    c.start()
    for p in pending + got_a + got_b:
        p.wait_send()
    c.wait()


def solution(mesh):
    nx, ny = mesh.shape["gx"], mesh.shape["gy"]

    def body(defect, coefficient):
        dma = pltpu.SemaphoreType.DMA
        scratch = []
        for l in range(3):
            scratch += [pltpu.VMEM((EX[l], EY[l], LANES), f32)] * 9
        scratch += [
            pltpu.VMEM((12, EY[0], LANES), f32),
            pltpu.VMEM((12, 72, LANES), f32),
            pltpu.VMEM((2, EX[2], EY[2], LANES), f32),
            pltpu.VMEM((8, LANES), f32),
            pltpu.VMEM((2, nx, 8, LANES), f32),
            pltpu.VMEM((nx, 8, LANES), f32),
            pltpu.VMEM((nx + 2, 8, LANES), f32),
            pltpu.VMEM((8 * ny, LANES), f32),
            pltpu.VMEM((8, LANES), f32),
            pltpu.VMEM((nx // 8, ny + 16, LANES), f32),
            dma((2,)),
            dma((16,)), dma((16,)), dma((16,)), dma((16,)), dma((16,)), dma((16,)),
            dma((3 * nx - 1,)), dma((3 * nx - 1,)), dma((2,)), dma((2,)), dma((ny - 1,)), dma((ny - 1,)),
        ]
        return pl.pallas_call(
            functools.partial(kernel, nx, ny),
            out_shape=jax.ShapeDtypeStruct(defect.shape, f32),
            in_specs=[pl.BlockSpec(memory_space=pl.ANY)] * 2,
            out_specs=pl.BlockSpec(memory_space=pl.ANY),
            scratch_shapes=scratch,
            compiler_params=pltpu.CompilerParams(
                collective_id=0, has_side_effects=True, vmem_limit_bytes=40 << 20
            ),
        )(defect, coefficient)

    placed = P("gx", "gy", None)
    return jax.shard_map(
        body, mesh=mesh, in_specs=(placed, placed), out_specs=placed, check_vma=False
    )
```

time: 473 us -> 66.7 us (0.14)
  the two profiles are of different devices: /device:TPU:132 before, /device:TPU:1 now
where the time goes in v1:
time: 66.7 us; the launch traced here: 66.5 us
  Pallas kernels  63.9 us (96%)
  local copies, waits for them, and re-layouts  2.6 us (4%)
    pallas_call x1, Pallas kernels, body(): pl.pallas_call(functools.partial(kernel, nx, ny), out_shape=jax.ShapeDtyp...  63.9 us
    unnamed x5, local copies, waits for them, and re-layouts  2.6 us

profile of v1, /device:TPU:1, one launch (start us, length us, event | category | flops | bytes accessed | tf_op | source)
XLA Modules:
  0.0 66.5 jit_solution(1989811812198228201)
XLA Ops:
  0.0 0.0 copy-start
  0.0 0.9 %copy-done = f32[16,32,128]{2,1,0:T(8,128)S(1)} copy-done((f32[16,32,128]{2,1,0:T(8,128)S(1)}, f32[16,32,128]{2,1,0:T(8,128)}, u32[]{:S(2)}) %copy-start) | copy-done | bytes 262168
  1.0 0.0 copy-start.1
  1.0 0.9 %copy-done.1 = f32[16,32,128]{2,1,0:T(8,128)S(1)} copy-done((f32[16,32,128]{2,1,0:T(8,128)S(1)}, f32[16,32,128]{2,1,0:T(8,128)}, u32[]{:S(2)}) %copy-start.1) | copy-done | bytes 262168
  1.9 63.9 %shard_map.28 = f32[16,32,128]{2,1,0:T(8,128)S(1)} custom-call(f32[16,32,128]{2,1,0:T(8,128)S(1)} %copy-done, f32[16,32,128]{2,1,0:T(8,128)S(1)} %copy-done.1), custom_call_target="tpu_custom_call" | custom-call | tf_op jit(solution)/shard_map/pallas_call | solution.py:614
  65.8 0.7 %copy.4 = f32[16,32,128]{2,1,0:T(8,128)} copy(f32[16,32,128]{2,1,0:T(8,128)S(1)} %shard_map.28) | data formatting | bytes 524288
Async XLA Ops:
  0.0 0.9 %copy-start = (f32[16,32,128]{2,1,0:T(8,128)S(1)}, f32[16,32,128]{2,1,0:T(8,128)}, u32[]{:S(2)}) copy-start(f32[16,32,128]{2,1,0:T(8,128)} %refs_0_.1) | copy-start | bytes 786436
  1.0 0.9 %copy-start.1 = (f32[16,32,128]{2,1,0:T(8,128)S(1)}, f32[16,32,128]{2,1,0:T(8,128)}, u32[]{:S(2)}) copy-start(f32[16,32,128]{2,1,0:T(8,128)} %refs_1_.1) | copy-start | bytes 786436

commit v2 on v1

--- a/solution.py
+++ b/solution.py
@@ -13,6 +13,7 @@
 COARSE_SWEEPS = 8
 LANES = 128
 f32 = jnp.float32
+U0W, U0S, U0R, U1W, U1S, U1R, U2W = 11, 10, 4, 11, 9, 4, 99
 
 BX, BY = (16, 8, 4), (32, 16, 8)
 HX, HY = (4, 8, 4), (4, 8, 4)
@@ -56,12 +57,41 @@
     return jnp.where(on, ahead(t, -(1 << b)), t)
 
 
-def loop(lo, hi, body, unroll=1):
-    def step(i, c):
-        body(i)
+def loop(lo, hi, body, unroll=1, carry=()):
+    rounds = (hi - lo) // unroll
+
+    def step(r, c):
+        for j in range(unroll):
+            c = body(lo + unroll * r + j, c)
         return c
 
-    lax.fori_loop(lo, hi, step, 0, unroll=unroll)
+    if rounds > 1:
+        carry = lax.fori_loop(0, rounds, step, carry)
+    else:
+        rounds = 0
+    for i in range(lo + unroll * rounds, hi):
+        carry = body(i, carry)
+    return carry
+
+
+K0, S0, K1, S1, GA, SV, GB, H3 = range(8)
+
+
+def phase_rows(nx, ny):
+    def rim(level, wx, wy):
+        bx, by = BX[level], BY[level]
+        return (bx + 2 * wx) * (by + 2 * wy) - bx * by
+
+    return (
+        rim(0, 4, 4),
+        rim(0, 3, 3),
+        rim(1, 8, 8),
+        rim(1, 6, 8),
+        2 * (3 * nx - 1),
+        2 * rim(2, 4, 4),
+        (ny - 1) * 2 * (nx // 8),
+        2 * nx,
+    )
 
 
 class Block:
@@ -107,11 +137,12 @@
         k0 = self.k[lo - 1] * self.inside(lo - 1)
         k1 = self.k[lo] * self.inside(lo)
         self.wx[lo - 1] = half * (k0 + k1)
-        lax.fori_loop(lo, hi, step, (k1, half * (k0 + k1)), unroll=unroll)
+        loop(lo, hi, step, unroll, (k1, half * (k0 + k1)))
 
     def first(self, src, dst, lo, hi, unroll=1):
-        def step(x):
+        def step(x, c):
             dst[x] = self.inv[x] * src[x]
+            return c
 
         loop(lo, hi, step, unroll)
 
@@ -124,9 +155,10 @@
         return c, (t + u) + w
 
     def sweep(self, s, src, dst, lo, hi, unroll=1, shift=0):
-        def step(x):
+        def step(x, carry):
             c, near = self.pull(src, x)
             dst[x - shift] = KEEP * c + self.inv[x] * (s[x] + near)
+            return carry
 
         loop(lo, hi, step, unroll)
 
@@ -137,12 +169,13 @@
     def restrict(self, plane, tmp, lo, pairs, row, count, put, unroll=1):
         lane = lane_iota((count, LANES))
 
-        def step(i):
+        def step(i, c):
             x = lo + 2 * i
             t = plane(x) + plane(x + 1)
             tmp[i, pl.ds(0, t.shape[0]), :] = t
             t = tmp[i, pl.ds(row, count, stride=2), :] + tmp[i, pl.ds(row + 1, count, stride=2), :]
             put(i, 0.125 * (t + swap(t, self.level)))
+            return c
 
         loop(0, pairs, step, unroll)
 
@@ -199,12 +232,12 @@
     s_in, k_in, out = refs[:3]
     level_refs = [refs[3 + 9 * l : 12 + 9 * l] for l in range(3)]
     (
-        tmp, rep, sv2, pack, acc, halo3, v3s, bcc, own4, v4s,
-        local_sem, s0_sems, r0_sems, s1_sems, r1_sems, s2_sems, r2_sems,
-        sa_sem, ra_sem, sh_sems, rh_sems, sb_sem, rb_sem,
+        tmp, rep, sv2, pack, acc, halo3, v3s, v3u, bcc, own4, v4s, ruler,
+        local_sem, out_sem, ssem, rsem, known,
     ) = refs[30:]
     gx, gy = lax.axis_index("gx"), lax.axis_index("gy")
     gh = nx // 8
+    ROWS = phase_rows(nx, ny)
 
     def there(dx, dy):
         return (lax.rem(gx + dx + nx, nx), lax.rem(gy + dy + ny, ny))
@@ -222,63 +255,80 @@
     column = [(i, j) for i in range(nx) for j in (-1, 0, 1) if (i, j) != (0, 0)]
     line = [(0, j) for j in range(1, ny)]
     column.sort(key=lambda o: -min(o[0], nx - o[0]))
-    peers = column + [(0, j) for j in range(2, ny - 1)]
     acc[...] = jnp.zeros_like(acc)
-    v3s[...] = jnp.zeros_like(v3s)
+    v3u[...] = jnp.zeros_like(v3u)
     barrier = pltpu.get_barrier_semaphore()
-    for dx, dy in peers:
+    for dx, dy in NEAR:
         pl.semaphore_signal(barrier, inc=1, device_id=there(dx, dy), device_id_type=MESH)
     for c in loads:
         c.wait()
 
+    pl.semaphore_wait(barrier, len(NEAR))
+
+    def remote(src, dst, phase, dx, dy):
+        c = pltpu.make_async_remote_copy(
+            src, dst, ssem.at[phase], rsem.at[phase], device_id=there(dx, dy), device_id_type=MESH
+        )
+        c.start()
+
+    def tell(step):
+        d = 1 << step
+        targets = [(0, d), (0, -d)]
+        if d <= nx // 4:
+            targets += [(d, 0), (-d, 0)]
+        for dx, dy in targets:
+            pl.semaphore_signal(known.at[step], inc=1, device_id=there(dx, dy), device_id_type=MESH)
+
+    def told(step):
+        pl.semaphore_wait(known.at[step], 4 if (1 << step) <= nx // 4 else 2)
+
+    def all_of(phase):
+        part = ruler.at[pl.ds(0, ROWS[phase]), :]
+        return pltpu.make_async_remote_copy(
+            part, part, ssem.at[phase], rsem.at[phase], device_id=there(1, 0), device_id_type=MESH
+        )
+
+    def received(phase):
+        all_of(phase).wait_recv()
+
+    def send(parts, phase):
+        for (dx, dy), (src, dst) in zip(NEAR, parts):
+            remote(src, dst, phase, dx, dy)
+
+    tell(0)
+    send(l0.slabs(l0.k, 4, 4), K0)
+    send(l0.slabs(l0.s, 3, 3), S0)
+
     def put_k1(i, t):
         l1.k[HX[1] + i, pl.ds(HY[1], BY[1]), :] = t
 
-    l0.restrict(lambda x: l0.k[x, own0[1], :], tmp, HX[0], BX[1], 0, BY[1], put_k1)
-
-    pl.semaphore_wait(barrier, len(peers))
-
-    pending = []
-
-    def send(parts, ssems, rsems, base=0):
-        copies = []
-        for i, (dx, dy) in enumerate(NEAR):
-            src, dst = parts[i]
-            c = pltpu.make_async_remote_copy(
-                src, dst, ssems.at[base + i], rsems.at[base + i], device_id=there(dx, dy), device_id_type=MESH
-            )
-            c.start()
-            copies.append(c)
-        pending.extend(copies)
-        return copies
-
-    got_k0 = send(l0.slabs(l0.k, 4, 4), s0_sems, r0_sems, 0)
-    got_s0 = send(l0.slabs(l0.s, 3, 3), s0_sems, r0_sems, 8)
-    got_k1 = send(l1.slabs(l1.k, 8, 8), s1_sems, r1_sems, 0)
-
-    for c in got_k0:
-        c.wait_recv()
-    l0.weights(1, EX[0] - 1)
-    for c in got_s0:
-        c.wait_recv()
-    l0.first(l0.s, l0.va, 1, EX[0] - 1)
-    l0.sweep(l0.s, l0.va, l0.vb, 2, EX[0] - 2)
+    l0.restrict(lambda x: l0.k[x, own0[1], :], tmp, HX[0], BX[1], 0, BY[1], put_k1, U0R)
+    send(l1.slabs(l1.k, 8, 8), K1)
+    told(0)
+    tell(1)
+
+    received(K0)
+    l0.weights(1, EX[0] - 1, U0W)
+    received(S0)
+    l0.first(l0.s, l0.va, 1, EX[0] - 1, U0W)
+    l0.sweep(l0.s, l0.va, l0.vb, 2, EX[0] - 2, U0S)
 
     def put_s1(i, t):
         l1.s[HX[1] + i, pl.ds(HY[1], BY[1]), :] = t
 
-    l0.restrict(lambda x: l0.residual(l0.s, l0.vb, x), tmp, HX[0], BX[1], HY[0], BY[1], put_s1)
-    got_s1 = send(l1.slabs(l1.s, 6, 8), s1_sems, r1_sems, 8)
-
-    for c in got_k1:
-        c.wait_recv()
+    l0.restrict(lambda x: l0.residual(l0.s, l0.vb, x), tmp, HX[0], BX[1], HY[0], BY[1], put_s1, U0R)
+    send(l1.slabs(l1.s, 6, 8), S1)
+    told(1)
+    tell(2)
+
+    received(K1)
 
     def put_k2(i, t):
         l2.k[i] = t
 
-    l1.restrict(lambda x: l1.k[x], tmp, 0, EX[2], 0, EY[2], put_k2)
-    l1.weights(1, EX[1] - 1)
-    l2.weights(1, EX[2] - 1)
+    l1.restrict(lambda x: l1.k[x], tmp, 0, EX[2], 0, EY[2], put_k2, 6)
+    l1.weights(1, EX[1] - 1, U1W)
+    l2.weights(1, EX[2] - 1, U2W)
 
     def packed(plane_ref):
         t = plane_ref[...]
@@ -289,45 +339,35 @@
     def put_pack(i, t):
         pack[pl.ds(4 * i, 4), :] = t
 
-    l2.restrict(lambda x: l2.k[x], tmp, HX[2], 2, HY[2], 4, put_pack, unroll=True)
+    l2.restrict(lambda x: l2.k[x], tmp, HX[2], 2, HY[2], 4, put_pack, unroll=99)
     acc[1, gx, pl.ds(1, 1), :] = packed(pack)
 
-    for c in got_s1:
-        c.wait_recv()
-    l1.first(l1.s, l1.va, 2, EX[1] - 2)
-    l1.sweep(l1.s, l1.va, l1.vb, 3, EX[1] - 3)
+    received(S1)
+    told(2)
+    tell(3)
+    l1.first(l1.s, l1.va, 2, EX[1] - 2, 10)
+    l1.sweep(l1.s, l1.va, l1.vb, 3, EX[1] - 3, U1S)
 
     def put_s2(i, t):
         l2.s[2 + i] = t
 
-    l1.restrict(lambda x: l1.residual(l1.s, l1.vb, x), tmp, 4, 8, 0, EY[2], put_s2)
-
-    l2.first(l2.s, l2.va, 2, EX[2] - 2, unroll=True)
-    l2.sweep(l2.s, l2.va, l2.vb, 3, EX[2] - 3, unroll=True)
-    l2.restrict(lambda x: l2.residual(l2.s, l2.vb, x), tmp, HX[2], 2, HY[2], 4, put_pack, unroll=True)
+    l1.restrict(lambda x: l1.residual(l1.s, l1.vb, x), tmp, 4, 8, 0, EY[2], put_s2, U1R)
+
+    l2.first(l2.s, l2.va, 2, EX[2] - 2, unroll=99)
+    l2.sweep(l2.s, l2.va, l2.vb, 3, EX[2] - 3, unroll=99)
+    l2.restrict(lambda x: l2.residual(l2.s, l2.vb, x), tmp, HX[2], 2, HY[2], 4, put_pack, unroll=99)
     acc[0, gx, pl.ds(1, 1), :] = packed(pack)
 
-    got_a = []
-    for n, (dx, dy) in enumerate(column):
-        c = pltpu.make_async_remote_copy(
-            acc.at[:, gx, pl.ds(1, 1), :],
-            acc.at[:, gx, pl.ds(1 - dy, 1), :],
-            sa_sem.at[n],
-            ra_sem.at[n],
-            device_id=there(dx, dy),
-            device_id_type=MESH,
-        )
-        c.start()
-        got_a.append(c)
+    for dx, dy in column:
+        remote(acc.at[:, gx, pl.ds(1, 1), :], acc.at[:, gx, pl.ds(1 - dy, 1), :], GA, dx, dy)
 
     own2 = (pl.ds(HX[2], BX[2]), pl.ds(HY[2], BY[2]))
     sv2[0, own2[0], own2[1], :] = l2.s[own2[0], own2[1], :]
     sv2[1, own2[0], own2[1], :] = l2.vb[own2[0], own2[1], :]
-    got_sv = send(l2.slabs(sv2.at[0], 4, 4), s2_sems, r2_sems, 0)
-    got_sv += send(l2.slabs(sv2.at[1], 4, 4), s2_sems, r2_sems, 8)
-
-    for c in got_a:
-        c.wait_recv()
+    for q in range(2):
+        send(l2.slabs(sv2.at[q], 4, 4), SV)
+
+    received(GA)
 
     shape = (nx, 8, LANES)
     lane = lane_iota(shape)
@@ -358,7 +398,7 @@
     s3 = acc[0]
     v = w3.inv * s3
     v = w3.sweep(s3, v)
-    v3s[pl.ds(1, nx)] = v
+    v3s[...] = v
     r3 = w3.residual(s3, v)
 
     def coarse4(t):
@@ -377,32 +417,18 @@
     mine = jnp.concatenate(coarse4(r3) + coarse4(acc[1]), axis=0)
     own4[pl.ds(0, 2 * gh), :] = mine
     bcc[pl.ds(pl.multiple_of(8 * gy, 8), 2 * gh), :] = mine
-    got_b = []
-    for n, (dx, dy) in enumerate(line):
-        c = pltpu.make_async_remote_copy(
+    told(3)
+    for dx, dy in line:
+        remote(
             own4.at[pl.ds(0, 2 * gh), :],
             bcc.at[pl.ds(pl.multiple_of(8 * gy, 8), 2 * gh), :],
-            sb_sem.at[n],
-            rb_sem.at[n],
-            device_id=there(dx, dy),
-            device_id_type=MESH,
-        )
-        c.start()
-        got_b.append(c)
-    got_h = []
-    for n, dy in enumerate((1, -1)):
-        c = pltpu.make_async_remote_copy(
-            v3s.at[pl.ds(1, nx), pl.ds(1, 1), :],
-            halo3.at[:, pl.ds(1 - dy, 1), :],
-            sh_sems.at[n],
-            rh_sems.at[n],
-            device_id=there(0, dy),
-            device_id_type=MESH,
-        )
-        c.start()
-        got_h.append(c)
-    for c in got_b:
-        c.wait_recv()
+            GB,
+            dx,
+            dy,
+        )
+    for dy in (1, -1):
+        remote(v3s.at[:, pl.ds(1, 1), :], halo3.at[:, pl.ds(1 - dy, 1), :], H3, 0, dy)
+    received(GB)
 
     s4 = jnp.stack([bcc[pl.ds(h, ny, stride=8), :] for h in range(gh)])
     k4 = jnp.stack([bcc[pl.ds(gh + h, ny, stride=8), :] for h in range(gh)])
@@ -517,8 +543,7 @@
     v4 = w4.sweep(s4, v4)
     v4s[:, pl.ds(8, ny), :] = v4
 
-    for c in got_h:
-        c.wait_recv()
+    received(H3)
     planes = []
     for h in range(gh):
         t = [v4s[h, pl.ds(7 + gy, 8), :]]
@@ -526,20 +551,17 @@
             t = [spread(q, b, value) for q in t for value in (0, 1)]
         planes += t
     sub = lax.broadcasted_iota(jnp.int32, (nx, 8, LANES), 1)
-    v = jnp.where(sub == 1, v3s[pl.ds(1, nx)], halo3[...]) + jnp.stack(planes)
+    v = jnp.where(sub == 1, v3s[...], halo3[...]) + jnp.stack(planes)
     v = jnp.where(in3, v, 0.0)
     v = w3.sweep(s3, v)
     v = w3.sweep(s3, v)
-    for c in got_h:
-        c.wait_send()
-    v3s[pl.ds(1, nx)] = v
-
-    for c in got_sv:
-        c.wait_recv()
+    v3u[pl.ds(1, nx)] = v
+
+    received(SV)
     shape = (8, LANES)
     lane, sub = lane_iota(shape), lax.broadcasted_iota(jnp.int32, shape, 0)
     for d in range(3):
-        t = v3s[gx + d]
+        t = v3u[gx + d]
         rows = [jnp.broadcast_to(t[i : i + 1], shape) for i in range(3)]
         rows = jnp.where(sub < 2, rows[0], jnp.where(sub < 6, rows[1], rows[2]))
         for xl in range(2):
@@ -553,10 +575,10 @@
             for e in range(2):
                 x = 2 * n + e
                 l2.va[x] = jnp.where(l2.inside(x) > 0, sv2[1, x] + t, 0.0)
-    l2.sweep(sv2.at[0], l2.va, l2.vb, 1, EX[2] - 1, unroll=True)
-    l2.sweep(sv2.at[0], l2.vb, l2.va, 2, EX[2] - 2, unroll=True)
-
-    def up1(i):
+    l2.sweep(sv2.at[0], l2.va, l2.vb, 1, EX[2] - 1, unroll=99)
+    l2.sweep(sv2.at[0], l2.vb, l2.va, 2, EX[2] - 2, unroll=99)
+
+    def up1(i, c):
         t = l2.va[i + 2]
         rep[i, pl.ds(0, EY[2], stride=2), :] = t
         rep[i, pl.ds(1, EY[2], stride=2), :] = t
@@ -564,12 +586,13 @@
         for e in range(2):
             x = 2 * i + 4 + e
             l1.va[x] = l1.vb[x] + t
-
-    loop(0, 8, up1)
-    l1.sweep(l1.s, l1.va, l1.vb, 6, EX[1] - 6)
-    l1.sweep(l1.s, l1.vb, l1.va, 7, EX[1] - 7)
-
-    def up0(i):
+        return c
+
+    loop(0, 8, up1, 4)
+    l1.sweep(l1.s, l1.va, l1.vb, 6, EX[1] - 6, 6)
+    l1.sweep(l1.s, l1.vb, l1.va, 7, EX[1] - 7, 5)
+
+    def up0(i, c):
         t = l1.va[i + 7]
         rep[i, pl.ds(4, EY[1], stride=2), :] = t
         rep[i, pl.ds(5, EY[1], stride=2), :] = t
@@ -577,15 +600,24 @@
         for e in range(2):
             x = 2 * i + 2 + e
             l0.va[x] = l0.vb[x] + t
-
-    loop(0, 10, up0)
-    l0.sweep(l0.s, l0.va, l0.vb, 3, EX[0] - 3)
-    l0.sweep(l0.s, l0.vb, l0.va, 4, EX[0] - 4)
-    c = pltpu.make_async_copy(l0.va.at[own0[0], own0[1], :], out, local_sem.at[0])
-    c.start()
-    for p in pending + got_a + got_b:
-        p.wait_send()
-    c.wait()
+        return c
+
+    loop(0, 10, up0, 5)
+    l0.sweep(l0.s, l0.va, l0.vb, 3, EX[0] - 3, 9)
+    chunk = BX[0] // 4
+    copies = []
+    for i in range(4):
+        lo = HX[0] + chunk * i
+        l0.sweep(l0.s, l0.vb, l0.va, lo, lo + chunk, chunk)
+        c = pltpu.make_async_copy(
+            l0.va.at[pl.ds(lo, chunk), own0[1], :], out.at[pl.ds(chunk * i, chunk)], out_sem.at[i]
+        )
+        c.start()
+        copies.append(c)
+    for phase in range(len(ROWS)):
+        all_of(phase).wait_send()
+    for c in copies:
+        c.wait()
 
 
 def solution(mesh):
@@ -593,6 +625,7 @@
 
     def body(defect, coefficient):
         dma = pltpu.SemaphoreType.DMA
+        rows = phase_rows(nx, ny)
         scratch = []
         for l in range(3):
             scratch += [pltpu.VMEM((EX[l], EY[l], LANES), f32)] * 9
@@ -603,22 +636,26 @@
             pltpu.VMEM((8, LANES), f32),
             pltpu.VMEM((2, nx, 8, LANES), f32),
             pltpu.VMEM((nx, 8, LANES), f32),
+            pltpu.VMEM((nx, 8, LANES), f32),
             pltpu.VMEM((nx + 2, 8, LANES), f32),
             pltpu.VMEM((8 * ny, LANES), f32),
             pltpu.VMEM((8, LANES), f32),
             pltpu.VMEM((nx // 8, ny + 16, LANES), f32),
+            pltpu.VMEM((max(rows), LANES), f32),
             dma((2,)),
-            dma((16,)), dma((16,)), dma((16,)), dma((16,)), dma((16,)), dma((16,)),
-            dma((3 * nx - 1,)), dma((3 * nx - 1,)), dma((2,)), dma((2,)), dma((ny - 1,)), dma((ny - 1,)),
+            dma((4,)),
+            dma((len(rows),)),
+            dma((len(rows),)),
+            pltpu.SemaphoreType.REGULAR((4,)),
         ]
         return pl.pallas_call(
             functools.partial(kernel, nx, ny),
             out_shape=jax.ShapeDtypeStruct(defect.shape, f32),
-            in_specs=[pl.BlockSpec(memory_space=pl.ANY)] * 2,
+            in_specs=[pl.BlockSpec(memory_space=pltpu.HBM)] * 2,
             out_specs=pl.BlockSpec(memory_space=pl.ANY),
             scratch_shapes=scratch,
             compiler_params=pltpu.CompilerParams(
-                collective_id=0, has_side_effects=True, vmem_limit_bytes=40 << 20
+                collective_id=0, has_side_effects=True, vmem_limit_bytes=54784 << 10
             ),
         )(defect, coefficient)
 

time: 66.7 us -> 49 us (0.73)
  Pallas kernels: 63.9 us -> 48.2 us
  local copies, waits for them, and re-layouts: 2.6 us -> 0.71 us
    pallas_call x1, Pallas kernels: 63.9 us -> 48.2 us  [body(): pl.pallas_call(functools.partial(kernel, nx, ny), out_shape=jax.ShapeDtyp...]
    unnamed x5 -> x1, local copies, waits for them, and re-layouts: 2.6 us -> 0.71 us
where the time goes in v2:
time: 49 us; the launch traced here: 48.9 us
  Pallas kernels  48.2 us (98%)
  local copies, waits for them, and re-layouts  0.71 us (1%)
    pallas_call x1, Pallas kernels, body(): pl.pallas_call(functools.partial(kernel, nx, ny), out_shape=jax.ShapeDtyp...  48.2 us

profile of v2, /device:TPU:1, one launch (start us, length us, event | category | flops | bytes accessed | tf_op | source)
XLA Modules:
  0.0 48.9 jit_solution(14994008973081164515)
XLA Ops:
  0.0 48.2 %shard_map.28 = f32[16,32,128]{2,1,0:T(8,128)S(1)} custom-call(f32[16,32,128]{2,1,0:T(8,128)} %refs_0_.1, f32[16,32,128]{2,1,0:T(8,128)} %refs_1_.1), custom_call_target="tpu_custom_call" | custom-call | tf_op jit(solution)/shard_map/pallas_call | solution.py:651
  48.2 0.7 %copy.4 = f32[16,32,128]{2,1,0:T(8,128)} copy(f32[16,32,128]{2,1,0:T(8,128)S(1)} %shard_map.28) | data formatting | bytes 524288

commit v3 on v2

--- a/solution.py
+++ b/solution.py
@@ -13,14 +13,14 @@
 COARSE_SWEEPS = 8
 LANES = 128
 f32 = jnp.float32
-U0W, U0S, U0R, U1W, U1S, U1R, U2W = 11, 10, 4, 11, 9, 4, 99
+U0W, U0S, U0R, U1W, U1S, U1R, U2W = 10, 9, 4, 11, 9, 4, 99
 
 BX, BY = (16, 8, 4), (32, 16, 8)
 HX, HY = (4, 8, 4), (4, 8, 4)
 EX = tuple(b + 2 * h for b, h in zip(BX, HX))
 EY = tuple(b + 2 * h for b, h in zip(BY, HY))
 
-NEAR = [(a, b) for a in (-1, 0, 1) for b in (-1, 0, 1) if (a, b) != (0, 0)]
+NEAR = [(1, 1), (1, -1), (-1, 1), (-1, -1), (1, 0), (-1, 0), (0, 1), (0, -1)]
 
 
 def ahead(t, d):
@@ -74,7 +74,7 @@
     return carry
 
 
-K0, S0, K1, S1, GA, SV, GB, H3 = range(8)
+K0, S0, K1, S1, GA, SV, GB, H3, V0 = range(9)
 
 
 def phase_rows(nx, ny):
@@ -83,14 +83,15 @@
         return (bx + 2 * wx) * (by + 2 * wy) - bx * by
 
     return (
-        rim(0, 4, 4),
         rim(0, 3, 3),
+        rim(0, 2, 2),
         rim(1, 8, 8),
-        rim(1, 6, 8),
+        rim(1, 6, 6),
         2 * (3 * nx - 1),
         2 * rim(2, 4, 4),
-        (ny - 1) * 2 * (nx // 8),
+        4 * (ny - 1),
         2 * nx,
+        rim(0, 2, 2),
     )
 
 
@@ -201,42 +202,39 @@
 
 
 class Whole:
-    def __init__(self, factor, k, near, masks, inside):
+    def __init__(self, factor, k, near, masks, inside=None):
         half = 0.5 * factor
         self.near = near
-        diag = None
-        self.w = []
+        faces, parts = [], []
         for n, mask in zip(near(k), masks):
             face = half * (k + n)
-            self.w.append(jnp.where(mask, face, 0.0))
-            face = jnp.where(mask, face, half * k)
-            diag = face if diag is None else diag + face
-        self.diag = diag
+            faces.append(jnp.where(mask, face, 0.0))
+            parts.append(jnp.where(mask, face, half * k))
+        diag = (parts[0] + parts[1]) + (parts[2] + parts[3]) + (parts[4] + parts[5])
         inv = DAMP / diag
         self.inv = inv if inside is None else jnp.where(inside, inv, 0.0)
+        self.w = [face * self.inv for face in faces]
+        self.back = diag * (1.0 / DAMP)
 
     def pull(self, v):
-        total = None
-        for n, w in zip(self.near(v), self.w):
-            total = w * n if total is None else total + w * n
-        return total
-
-    def sweep(self, s, v):
-        return KEEP * v + self.inv * (s + self.pull(v))
-
-    def residual(self, s, v):
-        return (s - self.diag * v) + self.pull(v)
+        t = [w * n for w, n in zip(self.w, self.near(v))]
+        return (t[0] + t[1]) + (t[2] + t[3]) + (t[4] + t[5])
+
+    def sweep(self, q, v):
+        return (KEEP * v + q) + self.pull(v)
+
+    def residual(self, q, v):
+        return ((q - DAMP * v) + self.pull(v)) * self.back
 
 
 def kernel(nx, ny, *refs):
     s_in, k_in, out = refs[:3]
     level_refs = [refs[3 + 9 * l : 12 + 9 * l] for l in range(3)]
     (
-        tmp, rep, sv2, pack, acc, halo3, v3s, v3u, bcc, own4, v4s, ruler,
+        tmp, rep, sv2, vh, pack, acc, halo3, v3s, v3u, bcc, own4, v4s, ruler,
         local_sem, out_sem, ssem, rsem, known,
     ) = refs[30:]
     gx, gy = lax.axis_index("gx"), lax.axis_index("gy")
-    gh = nx // 8
     ROWS = phase_rows(nx, ny)
 
     def there(dx, dy):
@@ -254,8 +252,8 @@
 
     column = [(i, j) for i in range(nx) for j in (-1, 0, 1) if (i, j) != (0, 0)]
     line = [(0, j) for j in range(1, ny)]
+    line.sort(key=lambda o: -sum(min(c % 4, -c % 4) for c in (o[1] // 2, o[1] // 8)))
     column.sort(key=lambda o: -min(o[0], nx - o[0]))
-    acc[...] = jnp.zeros_like(acc)
     v3u[...] = jnp.zeros_like(v3u)
     barrier = pltpu.get_barrier_semaphore()
     for dx, dy in NEAR:
@@ -296,8 +294,8 @@
             remote(src, dst, phase, dx, dy)
 
     tell(0)
-    send(l0.slabs(l0.k, 4, 4), K0)
-    send(l0.slabs(l0.s, 3, 3), S0)
+    send(l0.slabs(l0.k, 3, 3), K0)
+    send(l0.slabs(l0.s, 2, 2), S0)
 
     def put_k1(i, t):
         l1.k[HX[1] + i, pl.ds(HY[1], BY[1]), :] = t
@@ -308,18 +306,20 @@
     tell(1)
 
     received(K0)
-    l0.weights(1, EX[0] - 1, U0W)
+    l0.weights(2, EX[0] - 2, U0W)
     received(S0)
-    l0.first(l0.s, l0.va, 1, EX[0] - 1, U0W)
-    l0.sweep(l0.s, l0.va, l0.vb, 2, EX[0] - 2, U0S)
+    l0.first(l0.s, l0.va, 2, EX[0] - 2, U0W)
+    l0.sweep(l0.s, l0.va, l0.vb, 3, EX[0] - 3, U0S)
 
     def put_s1(i, t):
         l1.s[HX[1] + i, pl.ds(HY[1], BY[1]), :] = t
 
     l0.restrict(lambda x: l0.residual(l0.s, l0.vb, x), tmp, HX[0], BX[1], HY[0], BY[1], put_s1, U0R)
-    send(l1.slabs(l1.s, 6, 8), S1)
+    send(l1.slabs(l1.s, 6, 6), S1)
     told(1)
     tell(2)
+    for (dx, dy), (src, _), (_, dst) in zip(NEAR, l0.slabs(l0.vb, 2, 2), l0.slabs(vh, 2, 2)):
+        remote(src, dst, V0, dx, dy)
 
     received(K1)
 
@@ -340,7 +340,7 @@
         pack[pl.ds(4 * i, 4), :] = t
 
     l2.restrict(lambda x: l2.k[x], tmp, HX[2], 2, HY[2], 4, put_pack, unroll=99)
-    acc[1, gx, pl.ds(1, 1), :] = packed(pack)
+    acc[1, 1, pl.ds(gx, 1), :] = packed(pack)
 
     received(S1)
     told(2)
@@ -356,38 +356,32 @@
     l2.first(l2.s, l2.va, 2, EX[2] - 2, unroll=99)
     l2.sweep(l2.s, l2.va, l2.vb, 3, EX[2] - 3, unroll=99)
     l2.restrict(lambda x: l2.residual(l2.s, l2.vb, x), tmp, HX[2], 2, HY[2], 4, put_pack, unroll=99)
-    acc[0, gx, pl.ds(1, 1), :] = packed(pack)
+    acc[0, 1, pl.ds(gx, 1), :] = packed(pack)
 
     for dx, dy in column:
-        remote(acc.at[:, gx, pl.ds(1, 1), :], acc.at[:, gx, pl.ds(1 - dy, 1), :], GA, dx, dy)
-
-    own2 = (pl.ds(HX[2], BX[2]), pl.ds(HY[2], BY[2]))
-    sv2[0, own2[0], own2[1], :] = l2.s[own2[0], own2[1], :]
-    sv2[1, own2[0], own2[1], :] = l2.vb[own2[0], own2[1], :]
-    for q in range(2):
-        send(l2.slabs(sv2.at[q], 4, 4), SV)
+        remote(acc.at[:, 1, pl.ds(gx, 1), :], acc.at[:, 1 - dy, pl.ds(gx, 1), :], GA, dx, dy)
 
     received(GA)
 
-    shape = (nx, 8, LANES)
+    shape = (3, nx, LANES)
     lane = lane_iota(shape)
-    px = lax.broadcasted_iota(jnp.int32, shape, 0)
-    py = gy - 1 + lax.broadcasted_iota(jnp.int32, shape, 1)
+    px = lax.broadcasted_iota(jnp.int32, shape, 1)
+    py = gy - 1 + lax.broadcasted_iota(jnp.int32, shape, 0)
     b2, yl, z3 = bit(lane, 2), lane & 3, lane >> 3
 
     def near3(v):
         up, down = ahead(v, 4), ahead(v, -4)
         return (
-            jnp.where(b2, planes_ahead(down, 1), up),
-            jnp.where(b2, down, planes_ahead(up, -1)),
-            jnp.where(yl == 3, rows_ahead(ahead(v, -3), 1), ahead(v, 1)),
-            jnp.where(yl == 0, rows_ahead(ahead(v, 3), -1), ahead(v, -1)),
+            jnp.where(b2, rows_ahead(down, 1), up),
+            jnp.where(b2, down, rows_ahead(up, -1)),
+            jnp.where(yl == 3, planes_ahead(ahead(v, -3), 1), ahead(v, 1)),
+            jnp.where(yl == 0, planes_ahead(ahead(v, 3), -1), ahead(v, -1)),
             ahead(v, 8),
             ahead(v, -8),
         )
 
     x3, y3 = 2 * px + jnp.where(b2, 1, 0), 4 * py + yl
-    in3 = (py >= 0) & (py < ny) & (py < gy + 2)
+    in3 = (py >= 0) & (py < ny)
     w3 = Whole(
         0.25**3,
         jnp.where(in3, acc[1], 0.0),
@@ -395,174 +389,139 @@
         (x3 < 2 * nx - 1, x3 > 0, y3 < 4 * ny - 1, y3 > 0, z3 < 15, z3 > 0),
         in3,
     )
-    s3 = acc[0]
-    v = w3.inv * s3
-    v = w3.sweep(s3, v)
-    v3s[...] = v
-    r3 = w3.residual(s3, v)
+    q3 = w3.inv * acc[0]
+    v = w3.sweep(q3, q3)
+    v3s[...] = v[1]
+    r3 = w3.residual(q3, v)[1]
+
+    shape = (nx, LANES)
+    lane, sub = lane_iota(shape), lax.broadcasted_iota(jnp.int32, shape, 0)
+    place = ((lane >> 1) & 6) + (lane & 1) == (sub >> 1)
+    odd = (sub & 1) != 0
 
     def coarse4(t):
         t = t + swap(t, 2)
         t = t + swap(t, 0)
         t = 0.125 * (t + swap(t, 3))
-        on0, on2, on3 = (bit(lane_iota((8, LANES)), b) for b in (0, 2, 3))
-        rows = []
-        for h in range(gh):
-            p = [t[8 * h + i] for i in range(8)]
-            p = [jnp.where(on0, p[2 * i + 1], p[2 * i]) for i in range(4)]
-            p = [jnp.where(on2, p[2 * i + 1], p[2 * i]) for i in range(2)]
-            rows.append(jnp.where(on3, p[1], p[0])[1:2])
-        return rows
-
-    mine = jnp.concatenate(coarse4(r3) + coarse4(acc[1]), axis=0)
-    own4[pl.ds(0, 2 * gh), :] = mine
-    bcc[pl.ds(pl.multiple_of(8 * gy, 8), 2 * gh), :] = mine
+        t = jnp.where(place, t, 0.0)
+        return [jnp.sum(jnp.where(odd == h, t, 0.0), axis=0, keepdims=True) for h in (False, True)]
+
+    mine = jnp.concatenate(coarse4(r3) + coarse4(acc[1, 1]), axis=0)
+    own4[pl.ds(0, 4), :] = mine
+    bcc[pl.ds(pl.multiple_of(8 * gy, 8), 4), :] = mine
     told(3)
     for dx, dy in line:
-        remote(
-            own4.at[pl.ds(0, 2 * gh), :],
-            bcc.at[pl.ds(pl.multiple_of(8 * gy, 8), 2 * gh), :],
-            GB,
-            dx,
-            dy,
-        )
+        remote(own4.at[pl.ds(0, 4), :], bcc.at[pl.ds(pl.multiple_of(8 * gy, 8), 4), :], GB, dx, dy)
     for dy in (1, -1):
-        remote(v3s.at[:, pl.ds(1, 1), :], halo3.at[:, pl.ds(1 - dy, 1), :], H3, 0, dy)
+        remote(v3s, halo3.at[1 - dy], H3, 0, dy)
+    own2 = (pl.ds(HX[2], BX[2]), pl.ds(HY[2], BY[2]))
+    sv2[0, own2[0], own2[1], :] = l2.s[own2[0], own2[1], :]
+    sv2[1, own2[0], own2[1], :] = l2.vb[own2[0], own2[1], :]
+    for q in range(2):
+        send(l2.slabs(sv2.at[q], 4, 4), SV)
+
     received(GB)
 
-    s4 = jnp.stack([bcc[pl.ds(h, ny, stride=8), :] for h in range(gh)])
-    k4 = jnp.stack([bcc[pl.ds(gh + h, ny, stride=8), :] for h in range(gh)])
-    shape = (gh, ny, LANES)
+    s4 = jnp.stack([bcc[pl.ds(h, ny, stride=8), :] for h in range(2)])
+    k4 = jnp.stack([bcc[pl.ds(2 + h, ny, stride=8), :] for h in range(2)])
+    shape = (2, ny, LANES)
     lane = lane_iota(shape)
-    top = lax.broadcasted_iota(jnp.int32, shape, 0)
-    py = lax.broadcasted_iota(jnp.int32, shape, 1)
-    b0, b1, low = bit(lane, 0), bit(lane, 1), lane & 13
+    plane = lax.broadcasted_iota(jnp.int32, shape, 0)
+    b1 = bit(lane, 1)
+    y4, z4 = 2 * lax.broadcasted_iota(jnp.int32, shape, 1) + jnp.where(b1, 1, 0), lane >> 4
+    lane2, row = lane_iota((ny, LANES)), lax.broadcasted_iota(jnp.int32, (ny, LANES), 0)
+    c0 = bit(lane2, 0)
+
+    def plus(t):
+        return jnp.where(c0, ahead(t, 3), ahead(t, 1))
+
+    def minus(t):
+        return jnp.where(c0, ahead(t, -1), ahead(t, -3))
 
     def near4(v):
         up, down = ahead(v, 2), ahead(v, -2)
         return (
-            jnp.where(low == 13, planes_ahead(ahead(v, -13), 1), jnp.where(b0, ahead(v, 3), ahead(v, 1))),
-            jnp.where(low == 0, planes_ahead(ahead(v, 13), -1), jnp.where(b0, ahead(v, -1), ahead(v, -3))),
+            jnp.stack([v[1], plus(v[0])]),
+            jnp.stack([minus(v[1]), v[0]]),
             jnp.where(b1, rows_ahead(down, 1), up),
             jnp.where(b1, down, rows_ahead(up, -1)),
             ahead(v, 16),
             ahead(v, -16),
         )
 
-    y4, z4 = 2 * py + jnp.where(b1, 1, 0), lane >> 4
     w4 = Whole(
         0.25**4,
         k4,
         near4,
         (
-            (low < 13) | (top < gh - 1),
-            (low > 0) | (top > 0),
+            (lane & 13 < 13) | (plane < 1),
+            (lane & 13 > 0) | (plane > 0),
             y4 < 2 * ny - 1,
             y4 > 0,
             z4 < 7,
             z4 > 0,
         ),
-        None,
     )
 
     def coarse5(t):
+        t = t[0] + t[1]
+        t = t + swap(t, 1)
+        return 0.125 * (t + swap(t, 4))
+
+    def near5(v):
+        return plus(v), minus(v), rows_ahead(v, 1), rows_ahead(v, -1), ahead(v, 32), ahead(v, -32)
+
+    x5, z5 = lane2 & 13, lane2 >> 5
+    k5 = coarse5(k4)
+    w5 = Whole(0.25**5, k5, near5, (x5 < 13, x5 > 0, row < ny - 1, row > 0, z5 < 3, z5 > 0))
+
+    def coarse6(t):
         t = t + swap(t, 0)
-        t = t + swap(t, 1)
-        t = 0.125 * (t + swap(t, 4))
-        if gh == 1:
-            return t[0]
-        return jnp.where(bit(lane_iota((ny, LANES)), 0), t[1], t[0])
-
-    shape = (ny, LANES)
-    lane = lane_iota(shape)
-    row = lax.broadcasted_iota(jnp.int32, shape, 0)
-    mid, z5, z6 = lane & 12, lane >> 5, lane >> 6
-    c0, c3 = bit(lane, 0), bit(lane, 3)
-    end_hi = c0 if gh == 2 else lane >= 0
-    end_lo = ~c0 if gh == 2 else lane >= 0
-
-    def near5(v):
-        return (
-            jnp.where(mid == 12, ahead(v, -11), ahead(v, 4)),
-            jnp.where(mid == 0, ahead(v, 11), ahead(v, -4)),
-            rows_ahead(v, 1),
-            rows_ahead(v, -1),
-            ahead(v, 32),
-            ahead(v, -32),
-        )
+        t = t + swap(t, 5)
+        return 0.125 * (t + jnp.where((row & 1) != 0, rows_ahead(t, -1), rows_ahead(t, 1)))
 
     def near6(v):
-        return (
-            jnp.where(c3, ahead(v, -7), ahead(v, 8)),
-            jnp.where(c3, ahead(v, -8), ahead(v, 7)),
-            rows_ahead(v, 2),
-            rows_ahead(v, -2),
-            ahead(v, 64),
-            ahead(v, -64),
-        )
-
-    k5 = coarse5(k4)
-    w5 = Whole(
-        0.25**5,
-        k5,
-        near5,
-        (~((mid == 12) & end_hi), ~((mid == 0) & end_lo), row < ny - 1, row > 0, z5 < 3, z5 > 0),
-        None,
-    )
-
-    def coarse6(t):
-        t = t + swap(t, 2)
-        t = t + swap(t, 5)
-        odd = (row & 1) != 0
-        return 0.125 * (t + jnp.where(odd, rows_ahead(t, -1), rows_ahead(t, 1)))
-
-    w6 = Whole(
-        0.25**6,
-        coarse6(k5),
-        near6,
-        (~(c3 & end_hi), ~((~c3) & end_lo), row < ny - 2, row > 1, z6 < 1, z6 > 0),
-        None,
-    )
-
-    v4 = w4.inv * s4
-    v4 = w4.sweep(s4, v4)
-    s5 = coarse5(w4.residual(s4, v4))
-    v5 = w5.inv * s5
-    v5 = w5.sweep(s5, v5)
-    s6 = coarse6(w5.residual(s5, v5))
-    v6 = w6.inv * s6
-    v6 = lax.fori_loop(0, COARSE_SWEEPS - 1, lambda i, t: w6.sweep(s6, t), v6)
+        turned = ahead(v, 64)
+        return ahead(v, 4), ahead(v, -4), rows_ahead(v, 2), rows_ahead(v, -2), turned, turned
+
+    x6, z6 = (lane2 >> 2) & 3, lane2 >> 6
+    w6 = Whole(0.25**6, coarse6(k5), near6, (x6 < 3, x6 > 0, row < ny - 2, row > 1, z6 < 1, z6 > 0))
+
+    q4 = w4.inv * s4
+    v4 = w4.sweep(q4, q4)
+    q5 = w5.inv * coarse5(w4.residual(q4, v4))
+    v5 = w5.sweep(q5, q5)
+    q6 = w6.inv * coarse6(w5.residual(q5, v5))
+    v6 = q6
+    for _ in range(COARSE_SWEEPS - 1):
+        v6 = w6.sweep(q6, v6)
     v5 = v5 + v6
-    v5 = w5.sweep(s5, v5)
-    v5 = w5.sweep(s5, v5)
-    if gh == 1:
-        v4 = v4 + v5[None]
-    else:
-        v4 = v4 + jnp.stack([spread(v5, 0, 0), spread(v5, 0, 1)])
-    v4 = w4.sweep(s4, v4)
-    v4 = w4.sweep(s4, v4)
+    v5 = w5.sweep(q5, v5)
+    v5 = w5.sweep(q5, v5)
+    v4 = v4 + v5[None]
+    v4 = w4.sweep(q4, v4)
+    v4 = w4.sweep(q4, v4)
     v4s[:, pl.ds(8, ny), :] = v4
 
     received(H3)
-    planes = []
-    for h in range(gh):
-        t = [v4s[h, pl.ds(7 + gy, 8), :]]
-        for b in (3, 2, 0):
-            t = [spread(q, b, value) for q in t for value in (0, 1)]
-        planes += t
-    sub = lax.broadcasted_iota(jnp.int32, (nx, 8, LANES), 1)
-    v = jnp.where(sub == 1, v3s[...], halo3[...]) + jnp.stack(planes)
+    below = []
+    for g in range(3):
+        t = [jnp.broadcast_to(v4s[h, pl.ds(7 + gy + g, 1), :], (nx, LANES)) for h in range(2)]
+        t = jnp.where(place, jnp.where(odd, t[1], t[0]), 0.0)
+        for b in (0, 2, 3):
+            t = t + swap(t, b)
+        below.append(t)
+    v = jnp.stack([halo3[0], v3s[...], halo3[2]]) + jnp.stack(below)
     v = jnp.where(in3, v, 0.0)
-    v = w3.sweep(s3, v)
-    v = w3.sweep(s3, v)
-    v3u[pl.ds(1, nx)] = v
+    v = w3.sweep(q3, v)
+    v = w3.sweep(q3, v)
+    v3u[:, pl.ds(8, nx), :] = v
 
     received(SV)
     shape = (8, LANES)
     lane, sub = lane_iota(shape), lax.broadcasted_iota(jnp.int32, shape, 0)
     for d in range(3):
-        t = v3u[gx + d]
-        rows = [jnp.broadcast_to(t[i : i + 1], shape) for i in range(3)]
+        rows = [jnp.broadcast_to(v3u[g, pl.ds(7 + gx + d, 1), :], shape) for g in range(3)]
         rows = jnp.where(sub < 2, rows[0], jnp.where(sub < 6, rows[1], rows[2]))
         for xl in range(2):
             t = jnp.where((lane & 7) == 4 * xl + ((sub + 2) & 3), rows, 0.0)
@@ -592,6 +551,11 @@
     l1.sweep(l1.s, l1.va, l1.vb, 6, EX[1] - 6, 6)
     l1.sweep(l1.s, l1.vb, l1.va, 7, EX[1] - 7, 5)
 
+    received(V0)
+    all_of(V0).wait_send()
+    row = lax.broadcasted_iota(jnp.int32, (EY[0], LANES), 0)
+    mine0 = jnp.where((row >= HY[0]) & (row < HY[0] + BY[0]), 1.0, 0.0).astype(f32)
+
     def up0(i, c):
         t = l1.va[i + 7]
         rep[i, pl.ds(4, EY[1], stride=2), :] = t
@@ -599,25 +563,22 @@
         t = rep[i, pl.ds(16, EY[0]), :]
         for e in range(2):
             x = 2 * i + 2 + e
-            l0.va[x] = l0.vb[x] + t
+            own = mine0 * jnp.where((x >= HX[0]) & (x < HX[0] + BX[0]), 1.0, 0.0).astype(f32)
+            near = jnp.where(l0.inside(x) > 0, vh[x] + t, 0.0)
+            l0.va[x] = jnp.where(own > 0, l0.vb[x] + t, near)
         return c
 
     loop(0, 10, up0, 5)
     l0.sweep(l0.s, l0.va, l0.vb, 3, EX[0] - 3, 9)
-    chunk = BX[0] // 4
-    copies = []
-    for i in range(4):
-        lo = HX[0] + chunk * i
-        l0.sweep(l0.s, l0.vb, l0.va, lo, lo + chunk, chunk)
-        c = pltpu.make_async_copy(
-            l0.va.at[pl.ds(lo, chunk), own0[1], :], out.at[pl.ds(chunk * i, chunk)], out_sem.at[i]
-        )
-        c.start()
-        copies.append(c)
-    for phase in range(len(ROWS)):
+    def last(x, carry):
+        c, near = l0.pull(l0.vb, x)
+        t = KEEP * c + l0.inv[x] * (l0.s[x] + near)
+        out[x - HX[0]] = t[HY[0] : HY[0] + BY[0]]
+        return carry
+
+    loop(HX[0], HX[0] + BX[0], last, 8)
+    for phase in range(V0):
         all_of(phase).wait_send()
-    for c in copies:
-        c.wait()
 
 
 def solution(mesh):
@@ -633,14 +594,15 @@
             pltpu.VMEM((12, EY[0], LANES), f32),
             pltpu.VMEM((12, 72, LANES), f32),
             pltpu.VMEM((2, EX[2], EY[2], LANES), f32),
+            pltpu.VMEM((EX[0], EY[0], LANES), f32),
             pltpu.VMEM((8, LANES), f32),
-            pltpu.VMEM((2, nx, 8, LANES), f32),
-            pltpu.VMEM((nx, 8, LANES), f32),
-            pltpu.VMEM((nx, 8, LANES), f32),
-            pltpu.VMEM((nx + 2, 8, LANES), f32),
+            pltpu.VMEM((2, 3, nx, LANES), f32),
+            pltpu.VMEM((3, nx, LANES), f32),
+            pltpu.VMEM((nx, LANES), f32),
+            pltpu.VMEM((3, nx + 16, LANES), f32),
             pltpu.VMEM((8 * ny, LANES), f32),
             pltpu.VMEM((8, LANES), f32),
-            pltpu.VMEM((nx // 8, ny + 16, LANES), f32),
+            pltpu.VMEM((2, ny + 16, LANES), f32),
             pltpu.VMEM((max(rows), LANES), f32),
             dma((2,)),
             dma((4,)),
@@ -652,7 +614,7 @@
             functools.partial(kernel, nx, ny),
             out_shape=jax.ShapeDtypeStruct(defect.shape, f32),
             in_specs=[pl.BlockSpec(memory_space=pltpu.HBM)] * 2,
-            out_specs=pl.BlockSpec(memory_space=pl.ANY),
+            out_specs=pl.BlockSpec(memory_space=pltpu.VMEM),
             scratch_shapes=scratch,
             compiler_params=pltpu.CompilerParams(
                 collective_id=0, has_side_effects=True, vmem_limit_bytes=54784 << 10

time: 49 us -> 45.8 us (0.935)
  Pallas kernels: 48.2 us -> 45 us
    pallas_call x1, Pallas kernels: 48.2 us -> 45 us  [body(): pl.pallas_call(functools.partial(kernel, nx, ny), out_shape=jax.ShapeDtyp...]
where the time goes in v3:
time: 45.8 us; the launch traced here: 45.7 us
  Pallas kernels  45 us (98%)
  local copies, waits for them, and re-layouts  0.71 us (2%)
    pallas_call x1, Pallas kernels, body(): pl.pallas_call(functools.partial(kernel, nx, ny), out_shape=jax.ShapeDtyp...  45 us

profile of v3, /device:TPU:1, one launch (start us, length us, event | category | flops | bytes accessed | tf_op | source)
XLA Modules:
  0.0 45.7 jit_solution(15817799653141224704)
XLA Ops:
  0.0 45.0 %shard_map.28 = f32[16,32,128]{2,1,0:T(8,128)S(1)} custom-call(f32[16,32,128]{2,1,0:T(8,128)} %refs_0_.1, f32[16,32,128]{2,1,0:T(8,128)} %refs_1_.1), custom_call_target="tpu_custom_call" | custom-call | tf_op jit(solution)/shard_map/pallas_call | solution.py:613
  45.0 0.7 %copy.4 = f32[16,32,128]{2,1,0:T(8,128)} copy(f32[16,32,128]{2,1,0:T(8,128)S(1)} %shard_map.28) | data formatting | bytes 524288

commit v4 on v3

--- a/solution.py
+++ b/solution.py
@@ -16,7 +16,7 @@
 U0W, U0S, U0R, U1W, U1S, U1R, U2W = 10, 9, 4, 11, 9, 4, 99
 
 BX, BY = (16, 8, 4), (32, 16, 8)
-HX, HY = (4, 8, 4), (4, 8, 4)
+HX, HY = (4, 8, 4), (4, 16, 8)
 EX = tuple(b + 2 * h for b, h in zip(BX, HX))
 EY = tuple(b + 2 * h for b, h in zip(BY, HY))
 
@@ -74,23 +74,70 @@
     return carry
 
 
-K0, S0, K1, S1, GA, SV, GB, H3, V0 = range(9)
+ENTRY = NEAR + [(2, 0), (-2, 0)]
+ROUNDS = (
+    ((2, 0), (-2, 0), (0, 1), (0, -1)),
+    ((4, 0), (-4, 0), (0, 2), (0, -2)),
+    ((0, 4), (0, -4)),
+    ((0, 8), (0, -8)),
+)
+
+K0, S0, K1, S1, GA, SV, GB, H3, K0Y, S0Y, S1Y, V0 = range(12)
+
+
+def slabs(ref, halo, block, wide):
+    parts = []
+    for offset in NEAR:
+        spans = []
+        for d, h, b, w in zip(offset, halo, block, wide):
+            if d == 0:
+                spans.append((h, h, b))
+            elif d > 0:
+                spans.append((h + b - w, h - w, w))
+            else:
+                spans.append((h, h + b, w))
+        (sx, tx, cx), (sy, ty, cy) = spans
+        parts.append(
+            (
+                ref.at[pl.ds(sx, cx), pl.ds(sy, cy), :],
+                ref.at[pl.ds(tx, cx), pl.ds(ty, cy), :],
+            )
+        )
+    return parts
+
+
+def both(low, high):
+    return jnp.where(bit(lane_iota(low.shape), 0), high, low)
+
+
+def apart(t):
+    odd = bit(lane_iota(t.shape), 0)
+    return jnp.where(odd, ahead(t, -1), t), jnp.where(odd, t, ahead(t, 1))
 
 
 def phase_rows(nx, ny):
+    def beside(level, wy):
+        return BX[level] // (2 if level == 1 else 1) * 2 * wy
+
     def rim(level, wx, wy):
-        bx, by = BX[level], BY[level]
+        bx, by = BX[level] // (2 if level == 1 else 1), BY[level]
         return (bx + 2 * wx) * (by + 2 * wy) - bx * by
 
+    def ends(level, wx, wy):
+        return rim(level, wx, wy) - beside(level, wy)
+
     return (
-        rim(0, 3, 3),
-        rim(0, 2, 2),
-        rim(1, 8, 8),
-        rim(1, 6, 6),
-        2 * (3 * nx - 1),
+        ends(0, 3, 3),
+        ends(0, 2, 2),
+        rim(1, 4, 16),
+        ends(1, 3, 14),
+        5 * (nx - 1),
         2 * rim(2, 4, 4),
         4 * (ny - 1),
-        2 * nx,
+        4 * nx,
+        beside(0, 3),
+        beside(0, 2),
+        beside(1, 14),
         rim(0, 2, 2),
     )
 
@@ -180,26 +227,6 @@
 
         loop(0, pairs, step, unroll)
 
-    def slabs(self, ref, wx, wy):
-        parts = []
-        for dx, dy in NEAR:
-            spans = []
-            for d, h, b, w in ((dx, self.hx, self.bx, wx), (dy, self.hy, self.by, wy)):
-                if d == 0:
-                    spans.append((h, h, b))
-                elif d > 0:
-                    spans.append((h + b - w, h - w, w))
-                else:
-                    spans.append((h, h + b, w))
-            (sx, tx, cx), (sy, ty, cy) = spans
-            parts.append(
-                (
-                    ref.at[pl.ds(sx, cx), pl.ds(sy, cy), :],
-                    ref.at[pl.ds(tx, cx), pl.ds(ty, cy), :],
-                )
-            )
-        return parts
-
 
 class Whole:
     def __init__(self, factor, k, near, masks, inside=None):
@@ -231,7 +258,7 @@
     s_in, k_in, out = refs[:3]
     level_refs = [refs[3 + 9 * l : 12 + 9 * l] for l in range(3)]
     (
-        tmp, rep, sv2, vh, pack, acc, halo3, v3s, v3u, bcc, own4, v4s, ruler,
+        tmp, rep, sv2, vh, k1p, s1p, pack, acc, halo3, v3s, v3u, bcc, own4, v4s, ruler,
         local_sem, out_sem, ssem, rsem, known,
     ) = refs[30:]
     gx, gy = lax.axis_index("gx"), lax.axis_index("gy")
@@ -247,21 +274,42 @@
         pltpu.make_async_copy(k_in, l0.k.at[own0[0], own0[1], :], local_sem.at[0]),
         pltpu.make_async_copy(s_in, l0.s.at[own0[0], own0[1], :], local_sem.at[1]),
     ]
-    for c in loads:
-        c.start()
-
-    column = [(i, j) for i in range(nx) for j in (-1, 0, 1) if (i, j) != (0, 0)]
+
+    column = [(i, 0) for i in range(1, nx)]
     line = [(0, j) for j in range(1, ny)]
     line.sort(key=lambda o: -sum(min(c % 4, -c % 4) for c in (o[1] // 2, o[1] // 8)))
     column.sort(key=lambda o: -min(o[0], nx - o[0]))
-    v3u[...] = jnp.zeros_like(v3u)
     barrier = pltpu.get_barrier_semaphore()
-    for dx, dy in NEAR:
+    for dx, dy in ENTRY:
         pl.semaphore_signal(barrier, inc=1, device_id=there(dx, dy), device_id_type=MESH)
     for c in loads:
+        c.start()
+    v3u[...] = jnp.zeros_like(v3u)
+    for c in loads:
         c.wait()
 
-    pl.semaphore_wait(barrier, len(NEAR))
+    half1 = (HX[1] // 2, HY[1]), (BX[1] // 2, BY[1])
+
+    def put_k1(i, t):
+        l1.k[HX[1] + i, pl.ds(HY[1], BY[1]), :] = t
+
+    def pair_up(src, dst):
+        for i in range(BX[1] // 2):
+            x = HX[1] + 2 * i
+            low, high = (src[x + j, pl.ds(HY[1], BY[1]), :] for j in range(2))
+            dst[HX[1] // 2 + i, pl.ds(HY[1], BY[1]), :] = both(low, high)
+
+    def split(src, dst, lo, hi, unroll):
+        def step(i, c):
+            dst[2 * i], dst[2 * i + 1] = apart(src[i])
+            return c
+
+        loop(lo, hi, step, unroll)
+
+    l0.restrict(lambda x: l0.k[x, own0[1], :], tmp, HX[0], BX[1], 0, BY[1], put_k1, U0R)
+    pair_up(l1.k, k1p)
+
+    pl.semaphore_wait(barrier, len(ENTRY))
 
     def remote(src, dst, phase, dx, dy):
         c = pltpu.make_async_remote_copy(
@@ -270,15 +318,11 @@
         c.start()
 
     def tell(step):
-        d = 1 << step
-        targets = [(0, d), (0, -d)]
-        if d <= nx // 4:
-            targets += [(d, 0), (-d, 0)]
-        for dx, dy in targets:
+        for dx, dy in ROUNDS[step]:
             pl.semaphore_signal(known.at[step], inc=1, device_id=there(dx, dy), device_id_type=MESH)
 
     def told(step):
-        pl.semaphore_wait(known.at[step], 4 if (1 << step) <= nx // 4 else 2)
+        pl.semaphore_wait(known.at[step], len(ROUNDS[step]))
 
     def all_of(phase):
         part = ruler.at[pl.ds(0, ROWS[phase]), :]
@@ -289,39 +333,49 @@
     def received(phase):
         all_of(phase).wait_recv()
 
-    def send(parts, phase):
+    def send(parts, phase, phase_y=None):
         for (dx, dy), (src, dst) in zip(NEAR, parts):
-            remote(src, dst, phase, dx, dy)
+            remote(src, dst, phase if dx or phase_y is None else phase_y, dx, dy)
 
     tell(0)
-    send(l0.slabs(l0.k, 3, 3), K0)
-    send(l0.slabs(l0.s, 2, 2), S0)
-
-    def put_k1(i, t):
-        l1.k[HX[1] + i, pl.ds(HY[1], BY[1]), :] = t
-
-    l0.restrict(lambda x: l0.k[x, own0[1], :], tmp, HX[0], BX[1], 0, BY[1], put_k1, U0R)
-    send(l1.slabs(l1.k, 8, 8), K1)
+    send(slabs(l0.k, (HX[0], HY[0]), (BX[0], BY[0]), (3, 3)), K0, K0Y)
+    send(slabs(l0.s, (HX[0], HY[0]), (BX[0], BY[0]), (2, 2)), S0, S0Y)
+
+    send(slabs(k1p, half1[0], half1[1], (4, 16)), K1)
     told(0)
     tell(1)
 
+    def residual0(lo, pairs):
+        def put(i, t):
+            l1.s[HX[1] + (lo - HX[0]) // 2 + i, pl.ds(HY[1], BY[1]), :] = t
+
+        l0.restrict(lambda x: l0.residual(l0.s, l0.vb, x), tmp, lo, pairs, HY[0], BY[1], put, 4)
+
+    received(K0Y)
+    l0.weights(5, 19, 7)
+    received(S0Y)
+    l0.first(l0.s, l0.va, 5, 19, 7)
+    l0.sweep(l0.s, l0.va, l0.vb, 6, 18, 6)
+    residual0(8, 4)
     received(K0)
-    l0.weights(2, EX[0] - 2, U0W)
+    l0.weights(2, 5, 3)
+    l0.weights(19, 22, 3)
     received(S0)
-    l0.first(l0.s, l0.va, 2, EX[0] - 2, U0W)
-    l0.sweep(l0.s, l0.va, l0.vb, 3, EX[0] - 3, U0S)
-
-    def put_s1(i, t):
-        l1.s[HX[1] + i, pl.ds(HY[1], BY[1]), :] = t
-
-    l0.restrict(lambda x: l0.residual(l0.s, l0.vb, x), tmp, HX[0], BX[1], HY[0], BY[1], put_s1, U0R)
-    send(l1.slabs(l1.s, 6, 6), S1)
+    l0.first(l0.s, l0.va, 2, 5, 3)
+    l0.first(l0.s, l0.va, 19, 22, 3)
+    l0.sweep(l0.s, l0.va, l0.vb, 3, 6, 3)
+    l0.sweep(l0.s, l0.va, l0.vb, 18, 21, 3)
+    residual0(4, 2)
+    residual0(16, 2)
+    pair_up(l1.s, s1p)
+    send(slabs(s1p, half1[0], half1[1], (3, 14)), S1, S1Y)
     told(1)
     tell(2)
-    for (dx, dy), (src, _), (_, dst) in zip(NEAR, l0.slabs(l0.vb, 2, 2), l0.slabs(vh, 2, 2)):
+    for (dx, dy), (src, _), (_, dst) in zip(NEAR, slabs(l0.vb, (HX[0], HY[0]), (BX[0], BY[0]), (2, 2)), slabs(vh, (HX[0], HY[0]), (BX[0], BY[0]), (2, 2))):
         remote(src, dst, V0, dx, dy)
 
     received(K1)
+    split(k1p, l1.k, 0, EX[1] // 2, 6)
 
     def put_k2(i, t):
         l2.k[i] = t
@@ -330,37 +384,55 @@
     l1.weights(1, EX[1] - 1, U1W)
     l2.weights(1, EX[2] - 1, U2W)
 
-    def packed(plane_ref):
-        t = plane_ref[...]
-        lane = lane_iota(t.shape)
-        sub = lax.broadcasted_iota(jnp.int32, t.shape, 0)
-        return jnp.sum(jnp.where((lane & 7) == sub, t, 0.0), axis=0, keepdims=True)
+    def packed(count, base, blocks):
+        sub = lax.broadcasted_iota(jnp.int32, (count, LANES), 0)
+        lane = lane_iota((count, LANES))
+        low, high = (pack[i, pl.ds(0, count), :] for i in range(2))
+        y = (sub + base) & 3
+        t = jnp.where(lane & 7 == y, low, jnp.where(lane & 7 == 4 + y, high, 0.0))
+        on = (lane & 3) == y
+        return [jnp.sum(jnp.where(on & block(sub), t, 0.0), axis=0, keepdims=True) for block in blocks]
 
     def put_pack(i, t):
-        pack[pl.ds(4 * i, 4), :] = t
-
-    l2.restrict(lambda x: l2.k[x], tmp, HX[2], 2, HY[2], 4, put_pack, unroll=99)
-    acc[1, 1, pl.ds(gx, 1), :] = packed(pack)
-
+        pack[i, pl.ds(0, t.shape[0]), :] = t
+
+    l2.restrict(lambda x: l2.k[x], tmp, HX[2], 2, 0, 12, put_pack, unroll=99)
+    mine = pl.multiple_of(8 * gx, 8)
+    blocks = [lambda r, g=g: (r >> 2) == g for g in range(3)]
+    acc[pl.ds(mine + 2, 3), :] = jnp.concatenate(packed(16, 0, blocks), axis=0)
+
+    def residual1(lo, pairs):
+        def put(i, t):
+            l2.s[lo // 2 + i] = t
+
+        l1.restrict(lambda x: l1.residual(l1.s, l1.vb, x), tmp, lo, pairs, 0, EY[2], put, 3)
+
+    received(S1Y)
+    split(s1p, l1.s, 4, 8, 4)
+    l1.first(l1.s, l1.va, 8, 16, 8)
+    l1.sweep(l1.s, l1.va, l1.vb, 9, 15, 6)
+    residual1(10, 2)
     received(S1)
+    split(s1p, l1.s, 1, 4, 3)
+    split(s1p, l1.s, 8, 11, 3)
+    l1.first(l1.s, l1.va, 2, 8, 6)
+    l1.first(l1.s, l1.va, 16, 22, 6)
+    l1.sweep(l1.s, l1.va, l1.vb, 3, 9, 6)
+    l1.sweep(l1.s, l1.va, l1.vb, 15, 21, 6)
+    residual1(4, 3)
+    residual1(14, 3)
+
+    l2.first(l2.s, l2.va, 2, EX[2] - 2, unroll=99)
+    l2.sweep(l2.s, l2.va, l2.vb, 3, EX[2] - 3, unroll=99)
+    l2.restrict(lambda x: l2.residual(l2.s, l2.vb, x), tmp, HX[2], 2, HY[2] - 4, 8, put_pack, unroll=99)
+    blocks = [lambda r: (r >= 2) & (r < 6), lambda r: (r < 2) | (r >= 6)]
+    acc[pl.ds(mine, 2), :] = jnp.concatenate(packed(8, 2, blocks), axis=0)
+
+    for dx, dy in column:
+        remote(acc.at[pl.ds(mine, 5), :], acc.at[pl.ds(mine, 5), :], GA, dx, dy)
+
     told(2)
     tell(3)
-    l1.first(l1.s, l1.va, 2, EX[1] - 2, 10)
-    l1.sweep(l1.s, l1.va, l1.vb, 3, EX[1] - 3, U1S)
-
-    def put_s2(i, t):
-        l2.s[2 + i] = t
-
-    l1.restrict(lambda x: l1.residual(l1.s, l1.vb, x), tmp, 4, 8, 0, EY[2], put_s2, U1R)
-
-    l2.first(l2.s, l2.va, 2, EX[2] - 2, unroll=99)
-    l2.sweep(l2.s, l2.va, l2.vb, 3, EX[2] - 3, unroll=99)
-    l2.restrict(lambda x: l2.residual(l2.s, l2.vb, x), tmp, HX[2], 2, HY[2], 4, put_pack, unroll=99)
-    acc[0, 1, pl.ds(gx, 1), :] = packed(pack)
-
-    for dx, dy in column:
-        remote(acc.at[:, 1, pl.ds(gx, 1), :], acc.at[:, 1 - dy, pl.ds(gx, 1), :], GA, dx, dy)
-
     received(GA)
 
     shape = (3, nx, LANES)
@@ -382,16 +454,18 @@
 
     x3, y3 = 2 * px + jnp.where(b2, 1, 0), 4 * py + yl
     in3 = (py >= 0) & (py < ny)
+    own3, side3, *k3 = (acc[pl.ds(q, nx, stride=8), :] for q in range(5))
+    src3, k3 = jnp.stack([side3, own3, side3]), jnp.stack(k3)
     w3 = Whole(
         0.25**3,
-        jnp.where(in3, acc[1], 0.0),
+        jnp.where(in3, k3, 0.0),
         near3,
         (x3 < 2 * nx - 1, x3 > 0, y3 < 4 * ny - 1, y3 > 0, z3 < 15, z3 > 0),
         in3,
     )
-    q3 = w3.inv * acc[0]
+    q3 = w3.inv * src3
     v = w3.sweep(q3, q3)
-    v3s[...] = v[1]
+    v3s[0], v3s[1] = v[1], own3
     r3 = w3.residual(q3, v)[1]
 
     shape = (nx, LANES)
@@ -406,9 +480,9 @@
         t = jnp.where(place, t, 0.0)
         return [jnp.sum(jnp.where(odd == h, t, 0.0), axis=0, keepdims=True) for h in (False, True)]
 
-    mine = jnp.concatenate(coarse4(r3) + coarse4(acc[1, 1]), axis=0)
-    own4[pl.ds(0, 4), :] = mine
-    bcc[pl.ds(pl.multiple_of(8 * gy, 8), 4), :] = mine
+    mine4 = jnp.concatenate(coarse4(r3) + coarse4(k3[1]), axis=0)
+    own4[pl.ds(0, 4), :] = mine4
+    bcc[pl.ds(pl.multiple_of(8 * gy, 8), 4), :] = mine4
     told(3)
     for dx, dy in line:
         remote(own4.at[pl.ds(0, 4), :], bcc.at[pl.ds(pl.multiple_of(8 * gy, 8), 4), :], GB, dx, dy)
@@ -418,7 +492,7 @@
     sv2[0, own2[0], own2[1], :] = l2.s[own2[0], own2[1], :]
     sv2[1, own2[0], own2[1], :] = l2.vb[own2[0], own2[1], :]
     for q in range(2):
-        send(l2.slabs(sv2.at[q], 4, 4), SV)
+        send(slabs(sv2.at[q], (HX[2], HY[2]), (BX[2], BY[2]), (4, 4)), SV)
 
     received(GB)
 
@@ -511,7 +585,8 @@
         for b in (0, 2, 3):
             t = t + swap(t, b)
         below.append(t)
-    v = jnp.stack([halo3[0], v3s[...], halo3[2]]) + jnp.stack(below)
+    q3 = w3.inv * jnp.stack([halo3[0, 1], own3, halo3[2, 1]])
+    v = jnp.stack([halo3[0, 0], v3s[0], halo3[2, 0]]) + jnp.stack(below)
     v = jnp.where(in3, v, 0.0)
     v = w3.sweep(q3, v)
     v = w3.sweep(q3, v)
@@ -528,8 +603,8 @@
             for b in range(3):
                 t = t + swap(t, b)
             n = 2 * d + xl
-            rep[n, pl.ds(0, 8, stride=2), :] = t
-            rep[n, pl.ds(1, 8, stride=2), :] = t
+            rep[n, pl.ds(4, 8, stride=2), :] = t
+            rep[n, pl.ds(5, 8, stride=2), :] = t
             t = rep[n, pl.ds(0, EY[2]), :]
             for e in range(2):
                 x = 2 * n + e
@@ -557,9 +632,9 @@
     mine0 = jnp.where((row >= HY[0]) & (row < HY[0] + BY[0]), 1.0, 0.0).astype(f32)
 
     def up0(i, c):
-        t = l1.va[i + 7]
-        rep[i, pl.ds(4, EY[1], stride=2), :] = t
-        rep[i, pl.ds(5, EY[1], stride=2), :] = t
+        t = l1.va[i + 7, pl.ds(8, 32), :]
+        rep[i, pl.ds(4, 32, stride=2), :] = t
+        rep[i, pl.ds(5, 32, stride=2), :] = t
         t = rep[i, pl.ds(16, EY[0]), :]
         for e in range(2):
             x = 2 * i + 2 + e
@@ -591,14 +666,16 @@
         for l in range(3):
             scratch += [pltpu.VMEM((EX[l], EY[l], LANES), f32)] * 9
         scratch += [
-            pltpu.VMEM((12, EY[0], LANES), f32),
+            pltpu.VMEM((12, EY[1], LANES), f32),
             pltpu.VMEM((12, 72, LANES), f32),
             pltpu.VMEM((2, EX[2], EY[2], LANES), f32),
             pltpu.VMEM((EX[0], EY[0], LANES), f32),
-            pltpu.VMEM((8, LANES), f32),
-            pltpu.VMEM((2, 3, nx, LANES), f32),
-            pltpu.VMEM((3, nx, LANES), f32),
-            pltpu.VMEM((nx, LANES), f32),
+            pltpu.VMEM((EX[1] // 2, EY[1], LANES), f32),
+            pltpu.VMEM((EX[1] // 2, EY[1], LANES), f32),
+            pltpu.VMEM((2, 16, LANES), f32),
+            pltpu.VMEM((8 * nx, LANES), f32),
+            pltpu.VMEM((3, 2, nx, LANES), f32),
+            pltpu.VMEM((2, nx, LANES), f32),
             pltpu.VMEM((3, nx + 16, LANES), f32),
             pltpu.VMEM((8 * ny, LANES), f32),
             pltpu.VMEM((8, LANES), f32),

time: 45.8 us -> 43 us (0.939)
  Pallas kernels: 45 us -> 42.1 us
    pallas_call x1, Pallas kernels: 45 us -> 42.1 us  [body(): pl.pallas_call(functools.partial(kernel, nx, ny), out_shape=jax.ShapeDtyp...]
where the time goes in v4:
time: 43 us; the launch traced here: 42.8 us
  Pallas kernels  42.1 us (98%)
  local copies, waits for them, and re-layouts  0.71 us (2%)
    pallas_call x1, Pallas kernels, body(): pl.pallas_call(functools.partial(kernel, nx, ny), out_shape=jax.ShapeDtyp...  42.1 us

profile of v4, /device:TPU:1, one launch (start us, length us, event | category | flops | bytes accessed | tf_op | source)
XLA Modules:
  0.0 42.8 jit_solution(4459679163871146361)
XLA Ops:
  0.0 42.1 %shard_map.28 = f32[16,32,128]{2,1,0:T(8,128)S(1)} custom-call(f32[16,32,128]{2,1,0:T(8,128)} %refs_0_.1, f32[16,32,128]{2,1,0:T(8,128)} %refs_1_.1), custom_call_target="tpu_custom_call" | custom-call | tf_op jit(solution)/shard_map/pallas_call | solution.py:690
  42.1 0.7 %copy.4 = f32[16,32,128]{2,1,0:T(8,128)} copy(f32[16,32,128]{2,1,0:T(8,128)S(1)} %shard_map.28) | data formatting | bytes 524288

commit v5 on v4

--- a/solution.py
+++ b/solution.py
@@ -82,7 +82,7 @@
     ((0, 8), (0, -8)),
 )
 
-K0, S0, K1, S1, GA, SV, GB, H3, K0Y, S0Y, S1Y, V0 = range(12)
+K0, S0, K1, S1, GA, SV, GB, H3, K0Y, S0Y, S1Y, GK, KB, V0 = range(14)
 
 
 def slabs(ref, halo, block, wide):
@@ -131,13 +131,15 @@
         ends(0, 2, 2),
         rim(1, 4, 16),
         ends(1, 3, 14),
-        5 * (nx - 1),
+        2 * (nx - 1),
         2 * rim(2, 4, 4),
-        4 * (ny - 1),
+        2 * (ny - 1),
         4 * nx,
         beside(0, 3),
         beside(0, 2),
         beside(1, 14),
+        3 * (nx - 1),
+        2 * (ny - 1),
         rim(0, 2, 2),
     )
 
@@ -258,7 +260,7 @@
     s_in, k_in, out = refs[:3]
     level_refs = [refs[3 + 9 * l : 12 + 9 * l] for l in range(3)]
     (
-        tmp, rep, sv2, vh, k1p, s1p, pack, acc, halo3, v3s, v3u, bcc, own4, v4s, ruler,
+        tmp, rep, sv2, vh, k1p, s1p, pack, acc, acck, halo3, v3s, v3u, bcs, bck, own4, v4s, ruler,
         local_sem, out_sem, ssem, rsem, known,
     ) = refs[30:]
     gx, gy = lax.axis_index("gx"), lax.axis_index("gy")
@@ -299,9 +301,12 @@
             low, high = (src[x + j, pl.ds(HY[1], BY[1]), :] for j in range(2))
             dst[HX[1] // 2 + i, pl.ds(HY[1], BY[1]), :] = both(low, high)
 
-    def split(src, dst, lo, hi, unroll):
+    def split(src, dst, lo, hi, unroll, start=False):
         def step(i, c):
-            dst[2 * i], dst[2 * i + 1] = apart(src[i])
+            for x, t in zip((2 * i, 2 * i + 1), apart(src[i])):
+                dst[x] = t
+                if start:
+                    l1.va[x] = l1.inv[x] * t
             return c
 
         loop(lo, hi, step, unroll)
@@ -371,9 +376,6 @@
     send(slabs(s1p, half1[0], half1[1], (3, 14)), S1, S1Y)
     told(1)
     tell(2)
-    for (dx, dy), (src, _), (_, dst) in zip(NEAR, slabs(l0.vb, (HX[0], HY[0]), (BX[0], BY[0]), (2, 2)), slabs(vh, (HX[0], HY[0]), (BX[0], BY[0]), (2, 2))):
-        remote(src, dst, V0, dx, dy)
-
     received(K1)
     split(k1p, l1.k, 0, EX[1] // 2, 6)
 
@@ -399,7 +401,9 @@
     l2.restrict(lambda x: l2.k[x], tmp, HX[2], 2, 0, 12, put_pack, unroll=99)
     mine = pl.multiple_of(8 * gx, 8)
     blocks = [lambda r, g=g: (r >> 2) == g for g in range(3)]
-    acc[pl.ds(mine + 2, 3), :] = jnp.concatenate(packed(16, 0, blocks), axis=0)
+    acck[pl.ds(mine, 3), :] = jnp.concatenate(packed(16, 0, blocks), axis=0)
+    for dx, dy in column:
+        remote(acck.at[pl.ds(mine, 3), :], acck.at[pl.ds(mine, 3), :], GK, dx, dy)
 
     def residual1(lo, pairs):
         def put(i, t):
@@ -408,15 +412,12 @@
         l1.restrict(lambda x: l1.residual(l1.s, l1.vb, x), tmp, lo, pairs, 0, EY[2], put, 3)
 
     received(S1Y)
-    split(s1p, l1.s, 4, 8, 4)
-    l1.first(l1.s, l1.va, 8, 16, 8)
+    split(s1p, l1.s, 4, 8, 4, start=True)
     l1.sweep(l1.s, l1.va, l1.vb, 9, 15, 6)
     residual1(10, 2)
     received(S1)
-    split(s1p, l1.s, 1, 4, 3)
-    split(s1p, l1.s, 8, 11, 3)
-    l1.first(l1.s, l1.va, 2, 8, 6)
-    l1.first(l1.s, l1.va, 16, 22, 6)
+    split(s1p, l1.s, 1, 4, 3, start=True)
+    split(s1p, l1.s, 8, 11, 3, start=True)
     l1.sweep(l1.s, l1.va, l1.vb, 3, 9, 6)
     l1.sweep(l1.s, l1.va, l1.vb, 15, 21, 6)
     residual1(4, 3)
@@ -429,11 +430,11 @@
     acc[pl.ds(mine, 2), :] = jnp.concatenate(packed(8, 2, blocks), axis=0)
 
     for dx, dy in column:
-        remote(acc.at[pl.ds(mine, 5), :], acc.at[pl.ds(mine, 5), :], GA, dx, dy)
+        remote(acc.at[pl.ds(mine, 2), :], acc.at[pl.ds(mine, 2), :], GA, dx, dy)
 
     told(2)
     tell(3)
-    received(GA)
+    received(GK)
 
     shape = (3, nx, LANES)
     lane = lane_iota(shape)
@@ -454,8 +455,7 @@
 
     x3, y3 = 2 * px + jnp.where(b2, 1, 0), 4 * py + yl
     in3 = (py >= 0) & (py < ny)
-    own3, side3, *k3 = (acc[pl.ds(q, nx, stride=8), :] for q in range(5))
-    src3, k3 = jnp.stack([side3, own3, side3]), jnp.stack(k3)
+    k3 = jnp.stack([acck[pl.ds(q, nx, stride=8), :] for q in range(3)])
     w3 = Whole(
         0.25**3,
         jnp.where(in3, k3, 0.0),
@@ -463,11 +463,6 @@
         (x3 < 2 * nx - 1, x3 > 0, y3 < 4 * ny - 1, y3 > 0, z3 < 15, z3 > 0),
         in3,
     )
-    q3 = w3.inv * src3
-    v = w3.sweep(q3, q3)
-    v3s[0], v3s[1] = v[1], own3
-    r3 = w3.residual(q3, v)[1]
-
     shape = (nx, LANES)
     lane, sub = lane_iota(shape), lax.broadcasted_iota(jnp.int32, shape, 0)
     place = ((lane >> 1) & 6) + (lane & 1) == (sub >> 1)
@@ -480,24 +475,39 @@
         t = jnp.where(place, t, 0.0)
         return [jnp.sum(jnp.where(odd == h, t, 0.0), axis=0, keepdims=True) for h in (False, True)]
 
-    mine4 = jnp.concatenate(coarse4(r3) + coarse4(k3[1]), axis=0)
-    own4[pl.ds(0, 4), :] = mine4
-    bcc[pl.ds(pl.multiple_of(8 * gy, 8), 4), :] = mine4
+    def share4(rows, first, bcc, phase):
+        own4[pl.ds(first, 2), :] = rows
+        there4 = pl.ds(pl.multiple_of(8 * gy, 8), 2)
+        bcc[there4, :] = rows
+        for dx, dy in line:
+            remote(own4.at[pl.ds(first, 2), :], bcc.at[there4, :], phase, dx, dy)
+
     told(3)
-    for dx, dy in line:
-        remote(own4.at[pl.ds(0, 4), :], bcc.at[pl.ds(pl.multiple_of(8 * gy, 8), 4), :], GB, dx, dy)
+    share4(jnp.concatenate(coarse4(k3[1]), axis=0), 2, bck, KB)
+
+    received(GA)
+    own3, side3 = (acc[pl.ds(q, nx, stride=8), :] for q in range(2))
+    src3 = jnp.stack([side3, own3, side3])
+    q3 = w3.inv * src3
+    v = w3.sweep(q3, q3)
+    v3s[0], v3s[1] = v[1], own3
+    r3 = w3.residual(q3, v)[1]
+
+    share4(jnp.concatenate(coarse4(r3), axis=0), 0, bcs, GB)
     for dy in (1, -1):
         remote(v3s, halo3.at[1 - dy], H3, 0, dy)
+    for (dx, dy), (src, _), (_, dst) in zip(NEAR, slabs(l0.vb, (HX[0], HY[0]), (BX[0], BY[0]), (2, 2)), slabs(vh, (HX[0], HY[0]), (BX[0], BY[0]), (2, 2))):
+        remote(src, dst, V0, dx, dy)
+
     own2 = (pl.ds(HX[2], BX[2]), pl.ds(HY[2], BY[2]))
     sv2[0, own2[0], own2[1], :] = l2.s[own2[0], own2[1], :]
     sv2[1, own2[0], own2[1], :] = l2.vb[own2[0], own2[1], :]
     for q in range(2):
         send(slabs(sv2.at[q], (HX[2], HY[2]), (BX[2], BY[2]), (4, 4)), SV)
 
-    received(GB)
-
-    s4 = jnp.stack([bcc[pl.ds(h, ny, stride=8), :] for h in range(2)])
-    k4 = jnp.stack([bcc[pl.ds(2 + h, ny, stride=8), :] for h in range(2)])
+    received(KB)
+
+    k4 = jnp.stack([bck[pl.ds(h, ny, stride=8), :] for h in range(2)])
     shape = (2, ny, LANES)
     lane = lane_iota(shape)
     plane = lax.broadcasted_iota(jnp.int32, shape, 0)
@@ -561,6 +571,8 @@
     x6, z6 = (lane2 >> 2) & 3, lane2 >> 6
     w6 = Whole(0.25**6, coarse6(k5), near6, (x6 < 3, x6 > 0, row < ny - 2, row > 1, z6 < 1, z6 > 0))
 
+    received(GB)
+    s4 = jnp.stack([bcs[pl.ds(h, ny, stride=8), :] for h in range(2)])
     q4 = w4.inv * s4
     v4 = w4.sweep(q4, q4)
     q5 = w5.inv * coarse5(w4.residual(q4, v4))
@@ -674,9 +686,11 @@
             pltpu.VMEM((EX[1] // 2, EY[1], LANES), f32),
             pltpu.VMEM((2, 16, LANES), f32),
             pltpu.VMEM((8 * nx, LANES), f32),
+            pltpu.VMEM((8 * nx, LANES), f32),
             pltpu.VMEM((3, 2, nx, LANES), f32),
             pltpu.VMEM((2, nx, LANES), f32),
             pltpu.VMEM((3, nx + 16, LANES), f32),
+            pltpu.VMEM((8 * ny, LANES), f32),
             pltpu.VMEM((8 * ny, LANES), f32),
             pltpu.VMEM((8, LANES), f32),
             pltpu.VMEM((2, ny + 16, LANES), f32),

time: 43 us -> 42.6 us (level)
  no operation moved by 1% of the time
where the time goes in v5:
time: 42.6 us; the launch traced here: 42.4 us
  Pallas kernels  41.7 us (98%)
  local copies, waits for them, and re-layouts  0.71 us (2%)
    pallas_call x1, Pallas kernels, body(): pl.pallas_call(functools.partial(kernel, nx, ny), out_shape=jax.ShapeDtyp...  41.7 us

profile of v5, /device:TPU:1, one launch (start us, length us, event | category | flops | bytes accessed | tf_op | source)
XLA Modules:
  0.0 42.4 jit_solution(4479028160356247578)
XLA Ops:
  0.0 41.7 %shard_map.28 = f32[16,32,128]{2,1,0:T(8,128)S(1)} custom-call(f32[16,32,128]{2,1,0:T(8,128)} %refs_0_.1, f32[16,32,128]{2,1,0:T(8,128)} %refs_1_.1), custom_call_target="tpu_custom_call" | custom-call | tf_op jit(solution)/shard_map/pallas_call | solution.py:704
  41.7 0.7 %copy.4 = f32[16,32,128]{2,1,0:T(8,128)} copy(f32[16,32,128]{2,1,0:T(8,128)S(1)} %shard_map.28) | data formatting | bytes 524288

commit v6 on v5

--- a/solution.py
+++ b/solution.py
@@ -678,22 +678,22 @@
         for l in range(3):
             scratch += [pltpu.VMEM((EX[l], EY[l], LANES), f32)] * 9
         scratch += [
-            pltpu.VMEM((12, EY[1], LANES), f32),
+            pltpu.VMEM((12, EY[1] + 8, LANES), f32),
             pltpu.VMEM((12, 72, LANES), f32),
             pltpu.VMEM((2, EX[2], EY[2], LANES), f32),
             pltpu.VMEM((EX[0], EY[0], LANES), f32),
             pltpu.VMEM((EX[1] // 2, EY[1], LANES), f32),
             pltpu.VMEM((EX[1] // 2, EY[1], LANES), f32),
             pltpu.VMEM((2, 16, LANES), f32),
-            pltpu.VMEM((8 * nx, LANES), f32),
-            pltpu.VMEM((8 * nx, LANES), f32),
+            pltpu.VMEM((8 * nx + 8, LANES), f32),
+            pltpu.VMEM((8 * nx + 8, LANES), f32),
             pltpu.VMEM((3, 2, nx, LANES), f32),
             pltpu.VMEM((2, nx, LANES), f32),
-            pltpu.VMEM((3, nx + 16, LANES), f32),
-            pltpu.VMEM((8 * ny, LANES), f32),
-            pltpu.VMEM((8 * ny, LANES), f32),
-            pltpu.VMEM((8, LANES), f32),
-            pltpu.VMEM((2, ny + 16, LANES), f32),
+            pltpu.VMEM((3, nx + 24, LANES), f32),
+            pltpu.VMEM((8 * ny + 8, LANES), f32),
+            pltpu.VMEM((8 * ny + 8, LANES), f32),
+            pltpu.VMEM((16, LANES), f32),
+            pltpu.VMEM((2, ny + 24, LANES), f32),
             pltpu.VMEM((max(rows), LANES), f32),
             dma((2,)),
             dma((4,)),

time: 42.6 us -> 42.6 us (level)
  no operation moved by 1% of the time
where the time goes in v6:
time: 42.6 us; the launch traced here: 42.4 us
  Pallas kernels  41.7 us (98%)
  local copies, waits for them, and re-layouts  0.71 us (2%)
    pallas_call x1, Pallas kernels, body(): pl.pallas_call(functools.partial(kernel, nx, ny), out_shape=jax.ShapeDtyp...  41.7 us

profile of v6, /device:TPU:1, one launch (start us, length us, event | category | flops | bytes accessed | tf_op | source)
XLA Modules:
  0.0 42.4 jit_solution(14294162783603443280)
XLA Ops:
  0.0 41.7 %shard_map.28 = f32[16,32,128]{2,1,0:T(8,128)S(1)} custom-call(f32[16,32,128]{2,1,0:T(8,128)} %refs_0_.1, f32[16,32,128]{2,1,0:T(8,128)} %refs_1_.1), custom_call_target="tpu_custom_call" | custom-call | tf_op jit(solution)/shard_map/pallas_call | solution.py:704
  41.7 0.7 %copy.4 = f32[16,32,128]{2,1,0:T(8,128)} copy(f32[16,32,128]{2,1,0:T(8,128)S(1)} %shard_map.28) | data formatting | bytes 524288
